TPU v7x, 512 devices: a whole 4x8x8 slice. The times are simulated.
512 devices in a mesh: ctx: 64 (over y, x, core), fsdp: 8 (over z).
Axes of the slice: x: 4, y: 8, z: 8, core: 2. Of those that a mesh axis runs over, the one named last changes fastest.
Arguments:
- query_in: bfloat16 [8, 16384, 768], P('fsdp', 'ctx'), may hold values from -6 to 6
- key_in: bfloat16 [8, 16384, 768], P('fsdp', 'ctx'), may hold values from -6 to 6
- value_in: bfloat16 [8, 16384, 768], P('fsdp', 'ctx'), may hold values from -6 to 6
- out_grad: bfloat16 [8, 16384, 768], P('fsdp', 'ctx'), may hold values from -6 to 6
- w_out: bfloat16 [768, 768], P('fsdp'), may hold values from -0.21875 to 0.21875
- head_offsets: int32 [2, 12], replicated, may hold values from 0 to 1, as said below
- valid_tiles: int32 [8], P('fsdp'), may hold values from 4096 to 16384
Outputs:
- query_gradient: bfloat16 [8, 16384, 768], P('fsdp', 'ctx')
- key_gradient: bfloat16 [8, 16384, 768], P('fsdp', 'ctx')
- value_gradient: bfloat16 [8, 16384, 768], P('fsdp', 'ctx')
Inputs may be any that keep to these rules, and one draw needn't show every extreme that they name: head_offsets[b, h] lies below 2^b for every branch b.
All inputs are finite; a program needn't handle non-finite values.
Results may differ from a plain program's by a relative error of at most 0.012.
Values may be sent and summed in bfloat16 or wider, within the bound.
A program may use at most 128 MiB of HBM per device.

v0:
```python
import jax
import jax.numpy as jnp
from jax import lax
from jax.sharding import PartitionSpec as P

HEAD_COUNT = 12
NB = 2
BRANCH_ROWS = 1024


def swapped(block, axis, stride):
    count = lax.axis_size(axis)
    route = []
    for low in range(count):
        high = low | 1 << stride
        if high != low and high < count:
            route += [(low, high), (high, low)]
    return lax.ppermute(block, axis, route)


def gather_group(blocks, bit_count, device_idx):
    for bit_pos in range(bit_count):
        partner = swapped(blocks, "ctx", bit_pos)
        is_upper = device_idx >> bit_pos & 1 == 1
        blocks = jnp.where(
            is_upper,
            jnp.concatenate([partner, blocks], axis=1),
            jnp.concatenate([blocks, partner], axis=1),
        )
    return blocks


def return_group(blocks, bit_count, device_idx):
    for bit_pos in reversed(range(bit_count)):
        half_rows = blocks.shape[1] // 2
        take_upper = device_idx >> bit_pos & 1 == 1
        low_half = blocks[:, :half_rows]
        high_half = blocks[:, half_rows:]
        kept_half = jnp.where(take_upper, high_half, low_half)
        sent_half = jnp.where(take_upper, low_half, high_half)
        blocks = kept_half + swapped(sent_half, "ctx", bit_pos)
    return blocks


def spread_stat(stat, row_selector, fill_value):
    return jnp.where(row_selector[None], stat[:, None, :], fill_value).reshape(-1, stat.shape[1])


def pick_stat(full_stat, row_selector):
    reshaped_rows = full_stat.reshape(-1, row_selector.shape[0], full_stat.shape[1])
    return jnp.sum(jnp.where(row_selector[None], reshaped_rows, 0.0), axis=1)


def spread_rows(vectors, row_selector):
    spread_out = jnp.where(row_selector[None, :, :, None], vectors[:, None], 0.0)
    return spread_out.reshape(-1, vectors.shape[1], vectors.shape[2])


def on_device(query_in, key_in, value_in, out_grad, w_out, head_offsets, valid_tiles):
    segment_length = query_in.shape[1]
    model_width = query_in.shape[2]
    head_width = model_width // HEAD_COUNT
    logit_scale = head_width ** (-0.5)
    span_bits = (BRANCH_ROWS // segment_length).bit_length() - 1
    head_block = 4
    device_idx = lax.axis_index("ctx")
    valid_count = valid_tiles[0]
    positions = device_idx * segment_length + jnp.arange(segment_length, dtype=jnp.int32)
    grad_rows = out_grad[0]
    proj_grad = jnp.einsum(
        "td,kd->tk",
        grad_rows,
        lax.all_gather(w_out, "fsdp", axis=0, tiled=True),
        preferred_element_type=jnp.float32,
    )
    attn_grad = jnp.where((positions < valid_count)[:, None], proj_grad, 0.0).astype(jnp.bfloat16)
    sources = [query_in[0], key_in[0], value_in[0], attn_grad]
    layouts = []
    kv_local = []
    for branch_index in range(NB):
        dilation_rate = 2**branch_index
        row_total = segment_length // dilation_rate
        head_shifts = head_offsets[branch_index]
        row_selector = jnp.arange(dilation_rate, dtype=jnp.int32)[:, None] == head_shifts[None, :]
        one_hot = row_selector.astype(jnp.bfloat16)
        branch_parts = [
            jnp.einsum(
                "urhd,rh->uhd",
                source_row_list.reshape(row_total, dilation_rate, HEAD_COUNT, head_width),
                one_hot,
                preferred_element_type=jnp.float32,
            ).astype(jnp.bfloat16)
            for source_row_list in sources
        ]
        own_pos = (
            device_idx * segment_length
            + head_shifts[None, :]
            + dilation_rate * jnp.arange(row_total, dtype=jnp.int32)[:, None]
        )
        group_bits = span_bits + branch_index
        segment_begin = (device_idx >> group_bits) * (segment_length << group_bits)
        group_pos = (
            segment_begin
            + head_shifts[None, :]
            + dilation_rate * jnp.arange(BRANCH_ROWS, dtype=jnp.int32)[:, None]
        )
        layouts.append((row_selector, branch_parts, own_pos, group_pos))
        kv_local.append(
            jnp.stack([branch_parts[1], branch_parts[2]]).reshape(2, row_total, model_width)
        )
    kv_groups = [
        gather_group(kv_local[branch_index], span_bits + branch_index, device_idx)
        for branch_index in range(NB)
    ]
    key_groups = [
        kv_groups[branch_index][0].reshape(BRANCH_ROWS, HEAD_COUNT, head_width)
        for branch_index in range(NB)
    ]
    value_groups = [
        kv_groups[branch_index][1].reshape(BRANCH_ROWS, HEAD_COUNT, head_width)
        for branch_index in range(NB)
    ]
    grad_heads = attn_grad.reshape(segment_length, HEAD_COUNT, head_width)
    query_blocks = []
    term_parts = [[] for branch_index in range(NB)]
    for first_head in range(0, HEAD_COUNT, head_block):
        heads = slice(first_head, first_head + head_block)
        overall_maximum = jnp.full((segment_length, head_block), -jnp.inf, jnp.float32)
        score_list = []
        for branch_index in range(NB):
            row_selector, branch_parts, own_pos, group_pos = layouts[branch_index]
            attention_scores = (
                jnp.einsum(
                    "uhd,nhd->uhn",
                    branch_parts[0][:, heads],
                    key_groups[branch_index][:, heads],
                    preferred_element_type=jnp.float32,
                )
                * logit_scale
            )
            usable_rows = (group_pos[:, heads].T[None, :, :] < valid_count) | (
                own_pos[:, heads][:, :, None] >= valid_count
            )
            row_maximum = jnp.max(jnp.where(usable_rows, attention_scores, -jnp.inf), axis=2)
            overall_maximum = jnp.maximum(
                overall_maximum, spread_stat(row_maximum, row_selector[:, heads], -jnp.inf)
            )
            score_list.append((attention_scores, usable_rows))
        exponent_sum = jnp.zeros((segment_length, head_block), jnp.float32)
        for branch_index in range(NB):
            row_selector = layouts[branch_index][0][:, heads]
            attention_scores, usable_rows = score_list[branch_index]
            branch_maximum = pick_stat(overall_maximum, row_selector)
            gradient_terms = jnp.sum(
                jnp.where(usable_rows, jnp.exp(attention_scores - branch_maximum[:, :, None]), 0.0),
                axis=2,
            )
            exponent_sum = exponent_sum + spread_stat(gradient_terms, row_selector, 0.0)
        log_normalizer = overall_maximum + jnp.log(exponent_sum)
        attention_output = jnp.zeros((segment_length, head_block, head_width), jnp.float32)
        probability_list = []
        for branch_index in range(NB):
            row_selector = layouts[branch_index][0][:, heads]
            attention_scores, usable_rows = score_list[branch_index]
            branch_logsumexp = pick_stat(log_normalizer, row_selector)
            probabilities = jnp.where(
                usable_rows, jnp.exp(attention_scores - branch_logsumexp[:, :, None]), 0.0
            ).astype(jnp.bfloat16)
            probability_list.append((probabilities, branch_logsumexp))
            attention_output = attention_output + spread_rows(
                jnp.einsum(
                    "uhn,nhd->uhd",
                    probabilities,
                    value_groups[branch_index][:, heads],
                    preferred_element_type=jnp.float32,
                ),
                row_selector,
            )
        delta_rowsum = jnp.sum(grad_heads[:, heads].astype(jnp.float32) * attention_output, axis=2)
        query_block = jnp.zeros((segment_length, head_block, head_width), jnp.float32)
        for branch_index in range(NB):
            row_selector, branch_parts, own_pos, group_pos = layouts[branch_index]
            row_selector = row_selector[:, heads]
            probabilities, branch_logsumexp = probability_list[branch_index]
            delta_branch = pick_stat(delta_rowsum, row_selector)
            dprob = jnp.einsum(
                "uhd,nhd->uhn",
                branch_parts[3][:, heads],
                value_groups[branch_index][:, heads],
                preferred_element_type=jnp.float32,
            )
            score_gradient = (
                probabilities.astype(jnp.float32) * (dprob - delta_branch[:, :, None])
            ).astype(jnp.bfloat16)
            query_block = query_block + spread_rows(
                jnp.einsum(
                    "uhn,nhd->uhd",
                    score_gradient,
                    key_groups[branch_index][:, heads],
                    preferred_element_type=jnp.float32,
                )
                * logit_scale,
                row_selector,
            )
            key_terms = (
                jnp.einsum(
                    "uhn,uhd->nhd",
                    score_gradient,
                    branch_parts[0][:, heads],
                    preferred_element_type=jnp.float32,
                )
                * logit_scale
            )
            value_terms = jnp.einsum(
                "uhn,uhd->nhd",
                probabilities,
                branch_parts[3][:, heads],
                preferred_element_type=jnp.float32,
            )
            term_parts[branch_index].append(jnp.stack([key_terms, value_terms]))
        query_blocks.append(query_block)
    query_gradient = jnp.concatenate(query_blocks, axis=1)
    key_gradient = jnp.zeros((segment_length, HEAD_COUNT, head_width), jnp.float32)
    value_gradient = jnp.zeros((segment_length, HEAD_COUNT, head_width), jnp.float32)
    for branch_index in range(NB):
        row_selector, branch_parts, own_pos, group_pos = layouts[branch_index]
        row_total = branch_parts[0].shape[0]
        joined_terms = jnp.concatenate(term_parts[branch_index], axis=2).reshape(
            2, BRANCH_ROWS, model_width
        )
        summed = return_group(joined_terms, span_bits + branch_index, device_idx)
        key_own = summed[0].reshape(row_total, HEAD_COUNT, head_width)
        value_own = summed[1].reshape(row_total, HEAD_COUNT, head_width)
        key_gradient = key_gradient + spread_rows(key_own, row_selector)
        value_gradient = value_gradient + spread_rows(value_own, row_selector)
    return (
        query_gradient.reshape(1, segment_length, model_width).astype(jnp.bfloat16),
        key_gradient.reshape(1, segment_length, model_width).astype(jnp.bfloat16),
        value_gradient.reshape(1, segment_length, model_width).astype(jnp.bfloat16),
    )


def solution(mesh):
    in_specs = (
        P("fsdp", "ctx", None),
        P("fsdp", "ctx", None),
        P("fsdp", "ctx", None),
        P("fsdp", "ctx", None),
        P("fsdp", None),
        P(),
        P("fsdp"),
    )
    out_specs = (P("fsdp", "ctx", None), P("fsdp", "ctx", None), P("fsdp", "ctx", None))
    return jax.shard_map(
        on_device, mesh=mesh, in_specs=in_specs, out_specs=out_specs, check_vma=False
    )
```

profile of v0, /device:TPU:1, one launch (start us, length us, event | category | flops | bytes accessed | tf_op | source)
XLA Modules:
  0.0 586.1 jit_solution(4260196530865371285)
XLA Ops:
  7.9 2.1 copy.114
  31.3 22.6 %all-gather.2.cloned.1.call-done = bf16[768,768]{1,0:T(8,128)(2,1)} async-done(((bf16[96,768]{1,0:T(8,128)(2,1)}), bf16[768,768]{1,0:T(8,128)(2,1)}) %all-gather.2.cloned.1.call-update) | async-done | bytes 1179664 | tf_op jit(solution)/shard_map/all_gather | solution.py:73
  53.9 2.5 fusion.48
  58.4 3.0 multiply_convert_fusion
  63.1 6.5 %collective-permute-start = (bf16[2,256,768]{1,2,0:T(8,128)(2,1)}, bf16[2,256,768]{1,2,0:T(8,128)(2,1)}, u32[]{:S(2)}, u32[]{:S(2)}) collective-permute-start(bf16[2,256,768]{1,2,0:T(8,128)(2,1)} %pad_maximum_fusion), channel_id=1, source_target_pairs={{0,8},{8,0},{16,24},{24,16},{32,40},{40,32},{48,56},{56,48},{64,72... | collective-permute-start | bytes 2359304 | tf_op jit(solution)/shard_map/ppermute | solution.py:18
  70.9 2.5 reshape.820
  73.3 4.9 multiply_reduce_fusion
  81.1 2.0 maximum_select_fusion.2
  83.1 3.4 collective-permute-start.1
  86.6 2.2 collective-permute-start.2
  91.5 2.0 collective-permute-start.3
  96.7 41.5 %collective-permute-done.3 = bf16[2,256,768]{1,2,0:T(8,128)(2,1)} collective-permute-done((bf16[2,256,768]{1,2,0:T(8,128)(2,1)S(1)}, bf16[2,256,768]{1,2,0:T(8,128)(2,1)}, u32[]{:S(2)}, u32[]{:S(2)}) %collective-permute-start.3) | collective-permute-done | bytes 786464 | tf_op jit(solution)/shard_map/ppermute | solution.py:18
  138.1 2.2 maximum_select_fusion.3
  140.4 4.9 collective-permute-start.4
  145.3 2.9 maximum_select_fusion
  149.7 4.3 fusion.6
  155.5 4.2 fusion.3
  161.1 4.1 fusion
  166.7 12.3 %collective-permute-done.4 = bf16[2,512,768]{1,2,0:T(8,128)(2,1)} collective-permute-done((bf16[2,512,768]{1,2,0:T(8,128)(2,1)S(1)}, bf16[2,512,768]{1,2,0:T(8,128)(2,1)}, u32[]{:S(2)}, u32[]{:S(2)}) %collective-permute-start.4) | collective-permute-done | bytes 1572896 | tf_op jit(solution)/shard_map/ppermute | solution.py:18
  179.0 2.8 maximum_select_fusion.1
  182.5 2.6 fusion.27
  190.3 4.2 fusion.7
  199.2 3.4 fusion.28
  204.0 2.0 select_reduce_fusion.1
  207.5 3.8 fusion.29
  214.3 3.8 fusion.8
  220.9 1.9 broadcast_in_dim.592
  222.8 1.9 copy.166
  224.7 2.3 fusion.70
  229.7 3.3 fusion.24
  238.3 4.2 fusion.4
  247.2 3.4 fusion.25
  252.0 2.0 select_reduce_fusion.4
  255.5 3.8 fusion.26
  262.3 3.8 fusion.5
  270.8 1.9 copy.147
  272.7 2.3 fusion.71
  277.7 2.8 convolution_bitcast_fusion.3
  285.5 2.6 fusion.21
  293.4 4.2 fusion.1
  302.4 3.4 fusion.22
  307.2 2.0 select_reduce_fusion.7
  310.6 3.7 fusion.23
  317.5 4.3 fusion.2
  326.4 1.9 copy.128
  328.3 2.3 fusion.72
  333.3 2.9 convolution_bitcast_fusion.5
  336.2 2.7 convolution_bitcast_fusion.2
  372.6 2.4 slice_select_fusion
  376.5 5.0 collective-permute-start.7
  383.3 2.5 slice_select_fusion.1
  386.8 2.4 collective-permute-start.5
  393.8 54.5 %collective-permute-done.7 = f32[2,512,768]{1,2,0:T(8,128)} collective-permute-done((f32[2,512,768]{1,2,0:T(8,128)}, f32[2,512,768]{1,2,0:T(8,128)}, u32[]{:S(2)}, u32[]{:S(2)}) %collective-permute-start.7) | collective-permute-done | bytes 3145760 | tf_op jit(solution)/shard_map/ppermute | solution.py:18
  448.4 4.9 select_add_fusion
  455.5 3.2 collective-permute-start.8
  460.2 55.7 %collective-permute-done.5 = f32[2,512,768]{1,2,0:T(8,128)} collective-permute-done((f32[2,512,768]{1,2,0:T(8,128)}, f32[2,512,768]{1,2,0:T(8,128)}, u32[]{:S(2)}, u32[]{:S(2)}) %collective-permute-start.5) | collective-permute-done | bytes 3145760 | tf_op jit(solution)/shard_map/ppermute | solution.py:18
  516.0 4.9 select_add_fusion.1
  522.3 7.0 %collective-permute-start.6 = (f32[2,256,768]{1,2,0:T(8,128)}, f32[2,256,768]{1,2,0:T(8,128)}, u32[]{:S(2)}, u32[]{:S(2)}) collective-permute-start(f32[2,256,768]{1,2,0:T(8,128)} %slice_select_fusion.3), channel_id=1, source_target_pairs={{0,8},{8,0},{16,24},{24,16},{32,40},{40,32},{48,56},{56,48},{64,72... | collective-permute-start | bytes 4718600 | tf_op jit(solution)/shard_map/ppermute | solution.py:18
  530.3 19.4 %collective-permute-done.8 = f32[2,256,768]{1,2,0:T(8,128)} collective-permute-done((f32[2,256,768]{1,2,0:T(8,128)}, f32[2,256,768]{1,2,0:T(8,128)}, u32[]{:S(2)}, u32[]{:S(2)}) %collective-permute-start.8) | collective-permute-done | bytes 1572896 | tf_op jit(solution)/shard_map/ppermute | solution.py:18
  552.5 4.6 collective-permute-start.9
  558.7 3.0 select_add_fusion.3
  567.7 2.3 copy.189
  571.6 2.4 copy.187
  574.0 2.1 fusion.79
  (350 shorter events, 177.5 us)
Async XLA Ops:
  7.2 46.8 %copy-start = (bf16[1,256,768]{2,1,0:T(8,128)(2,1)S(1)}, bf16[1,256,768]{2,1,0:T(8,128)(2,1)}, u32[]{:S(2)}) copy-start(bf16[1,256,768]{2,1,0:T(8,128)(2,1)} %param.10) | copy-start | bytes 1179652
  7.2 4.5 copy-start.46
  7.2 46.7 %all-gather.2.cloned.1.call-start = ((), (), s32[]{:S(2)}) async-start(), calls=%async_computation | async-start | bytes 1327104 | tf_op jit(solution)/shard_map/all_gather | solution.py:73
  10.0 3.4 copy-start.47
  12.8 4.0 copy-start.91
  18.0 12.6 %copy-start.77 = (pred[2,4]{1,0:T(4,128)(4,1)}, pred[2,4]{1,0:T(4,128)(4,1)S(1)}, u32[]{:S(2)}) copy-start(pred[2,4]{1,0:T(4,128)(4,1)S(1)} %get-tuple-element.49) | copy-start | bytes 28
  18.0 12.6 %copy-start.79 = (pred[2,4]{1,0:T(4,128)(4,1)}, pred[2,4]{1,0:T(4,128)(4,1)S(1)}, u32[]{:S(2)}) copy-start(pred[2,4]{1,0:T(4,128)(4,1)S(1)} %get-tuple-element.48) | copy-start | bytes 28
  58.4 11.8 %copy-start.94 = (s32[12]{0:T(128)S(1)}, s32[12]{0:T(128)}, u32[]{:S(2)}) copy-start(s32[12]{0:T(128)} %get-tuple-element.40) | copy-start | bytes 148
  63.1 17.9 %collective-permute-start = (bf16[2,256,768]{1,2,0:T(8,128)(2,1)}, bf16[2,256,768]{1,2,0:T(8,128)(2,1)}, u32[]{:S(2)}, u32[]{:S(2)}) collective-permute-start(bf16[2,256,768]{1,2,0:T(8,128)(2,1)} %pad_maximum_fusion), channel_id=1, source_target_pairs={{0,8},{8,0},{16,24},{24,16},{32,40},{40,32},{48,56},{56,48},{64,72... | collective-permute-start | bytes 2359304 | tf_op jit(solution)/shard_map/ppermute | solution.py:18
  81.0 8.5 %copy-start.42 = (bf16[12,128,64]{1,2,0:T(8,128)(2,1)}, bf16[12,128,64]{1,2,0:T(8,128)(2,1)S(1)}, u32[]{:S(2)}) copy-start(bf16[12,128,64]{1,2,0:T(8,128)(2,1)S(1)} %copy.199) | copy-start | bytes 589828
  81.0 7.8 %copy-start.84 = (pred[1,12]{1,0:T(4,128)(4,1)S(1)}, pred[1,12]{1,0:T(4,128)(4,1)}, u32[]{:S(2)}) copy-start(pred[1,12]{1,0:T(4,128)(4,1)} %get-tuple-element.38) | copy-start | bytes 40
  81.0 7.8 %copy-start.65 = (s32[256,12]{0,1:T(8,128)S(1)}, s32[256,12]{0,1:T(8,128)}, u32[]{:S(2)}) copy-start(s32[256,12]{0,1:T(8,128)} %iota_add_fusion.1) | copy-start | bytes 36868
  81.0 12.5 %copy-start.92 = (s32[12]{0:T(128)S(1)}, s32[12]{0:T(128)}, u32[]{:S(2)}) copy-start(s32[12]{0:T(128)} %get-tuple-element.39) | copy-start | bytes 148
  81.0 12.5 %copy-start.93 = (s32[12]{0:T(128)S(1)}, s32[12]{0:T(128)}, u32[]{:S(2)}) copy-start(s32[12]{0:T(128)} %get-tuple-element.41) | copy-start | bytes 148
  83.1 13.1 %copy-start.41 = (bf16[12,128,64]{2,0,1:T(8,128)(2,1)S(1)}, bf16[12,128,64]{2,0,1:T(8,128)(2,1)}, u32[]{:S(2)}) copy-start(bf16[12,128,64]{2,0,1:T(8,128)(2,1)} %get-tuple-element.14) | copy-start | bytes 589828
  83.1 62.2 %collective-permute-start.1 = (bf16[2,512,768]{1,2,0:T(8,128)(2,1)S(1)}, bf16[2,512,768]{1,2,0:T(8,128)(2,1)}, u32[]{:S(2)}, u32[]{:S(2)}) collective-permute-start(bf16[2,512,768]{1,2,0:T(8,128)(2,1)S(1)} %maximum_select_fusion.2), channel_id=1, source_target_pairs={{0,16},{16,0},{8,24},{24,8},{32,48},{48,32},{40,56},{56,40},{64,80... | collective-permute-start | bytes 4718600 | tf_op jit(solution)/shard_map/ppermute | solution.py:18
  86.6 3.6 collective-permute-start.2
  91.5 5.2 copy-start.28
  91.5 46.6 %collective-permute-start.3 = (bf16[2,256,768]{1,2,0:T(8,128)(2,1)S(1)}, bf16[2,256,768]{1,2,0:T(8,128)(2,1)}, u32[]{:S(2)}, u32[]{:S(2)}) collective-permute-start(bf16[2,256,768]{1,2,0:T(8,128)(2,1)S(1)} %maximum_select_fusion.4), channel_id=1, source_target_pairs={{0,16},{16,0},{8,24},{24,8},{32,48},{48,32},{40,56},{56,40},{64,80... | collective-permute-start | bytes 2359304 | tf_op jit(solution)/shard_map/ppermute | solution.py:18
  140.4 38.6 %collective-permute-start.4 = (bf16[2,512,768]{1,2,0:T(8,128)(2,1)S(1)}, bf16[2,512,768]{1,2,0:T(8,128)(2,1)}, u32[]{:S(2)}, u32[]{:S(2)}) collective-permute-start(bf16[2,512,768]{1,2,0:T(8,128)(2,1)S(1)} %maximum_select_fusion.3), channel_id=1, source_target_pairs={{0,32},{32,0},{8,40},{40,8},{16,48},{48,16},{24,56},{56,24},{64,96... | collective-permute-start | bytes 4718600 | tf_op jit(solution)/shard_map/ppermute | solution.py:18
  149.7 11.5 %copy-start.6 = (bf16[1,1024,768]{1,2,0:T(8,128)(2,1)}, bf16[1,1024,768]{1,2,0:T(8,128)(2,1)S(1)}, u32[]{:S(2)}) copy-start(bf16[1,1024,768]{1,2,0:T(8,128)(2,1)S(1)} %get-tuple-element.19) | copy-start | bytes 4718596
  207.5 3.8 copy-start.55
  214.3 3.8 copy-start.10
  255.5 3.8 copy-start.56
  262.3 3.8 copy-start.11
  277.7 4.3 copy-start.35
  277.7 4.3 copy-start.64
  310.6 3.8 copy-start.57
  317.5 4.3 copy-start.13
  341.2 4.4 copy-start.43
  353.2 4.4 copy-start.44
  367.2 3.9 copy-start.20
  371.7 9.8 %copy-start.31 = (bf16[256,4,1024]{0,2,1:T(8,128)(2,1)}, bf16[256,4,1024]{0,2,1:T(8,128)(2,1)S(1)}, u32[]{:S(2)}) copy-start(bf16[256,4,1024]{0,2,1:T(8,128)(2,1)S(1)} %fusion.18) | copy-start | bytes 6291460
  372.6 3.9 copy-start.3
  372.6 9.0 %copy-start.63 = (bf16[256,12,64]{0,2,1:T(8,128)(2,1)S(1)}, bf16[256,12,64]{0,2,1:T(8,128)(2,1)}, u32[]{:S(2)}) copy-start(bf16[256,12,64]{0,2,1:T(8,128)(2,1)} %get-tuple-element.52) | copy-start | bytes 1179652
  372.6 9.7 %copy-start.51 = (f32[1,1024,4,64]{1,3,2,0:T(8,128)S(1)}, f32[1,1024,4,64]{1,3,2,0:T(8,128)}, u32[]{:S(2)}) copy-start(f32[1,1024,4,64]{1,3,2,0:T(8,128)} %fusion.45) | copy-start | bytes 3145732
  372.6 9.7 %copy-start.52 = (f32[1,1024,4,64]{1,3,2,0:T(8,128)S(1)}, f32[1,1024,4,64]{1,3,2,0:T(8,128)}, u32[]{:S(2)}) copy-start(f32[1,1024,4,64]{1,3,2,0:T(8,128)} %fusion.46) | copy-start | bytes 3145732
  376.5 5.8 copy-start.48
  376.5 5.8 copy-start.49
  376.5 5.8 copy-start.50
  376.5 71.9 %collective-permute-start.7 = (f32[2,512,768]{1,2,0:T(8,128)}, f32[2,512,768]{1,2,0:T(8,128)}, u32[]{:S(2)}, u32[]{:S(2)}) collective-permute-start(f32[2,512,768]{1,2,0:T(8,128)} %slice_select_fusion), channel_id=1, source_target_pairs={{0,32},{32,0},{8,40},{40,8},{16,48},{48,16},{24,56},{56,24},{64,96... | collective-permute-start | bytes 9437192 | tf_op jit(solution)/shard_map/ppermute | solution.py:18
  383.2 3.6 copy-start.2
  383.2 6.0 %copy-start.95 = (pred[12]{0:T(512)(128)(4,1)S(1)}, pred[12]{0:T(512)(128)(4,1)}, u32[]{:S(2)}) copy-start(pred[12]{0:T(512)(128)(4,1)} %get-tuple-element.36) | copy-start | bytes 40
  383.2 6.7 %copy-start.82 = (pred[2,12]{1,0:T(4,128)(4,1)S(1)}, pred[2,12]{1,0:T(4,128)(4,1)}, u32[]{:S(2)}) copy-start(pred[2,12]{1,0:T(4,128)(4,1)} %copy-done.81) | copy-start | bytes 76
  383.3 7.5 %copy-start.23 = (bf16[128,4,1024]{0,2,1:T(8,128)(2,1)S(1)}, bf16[128,4,1024]{0,2,1:T(8,128)(2,1)}, u32[]{:S(2)}) copy-start(bf16[128,4,1024]{0,2,1:T(8,128)(2,1)} %copy-done.22) | copy-start | bytes 3145732
  386.8 129.1 %collective-permute-start.5 = (f32[2,512,768]{1,2,0:T(8,128)}, f32[2,512,768]{1,2,0:T(8,128)}, u32[]{:S(2)}, u32[]{:S(2)}) collective-permute-start(f32[2,512,768]{1,2,0:T(8,128)} %slice_select_fusion.1), channel_id=1, source_target_pairs={{0,16},{16,0},{8,24},{24,8},{32,48},{48,32},{40,56},{56,40},{64,80... | collective-permute-start | bytes 9437192 | tf_op jit(solution)/shard_map/ppermute | solution.py:18
  453.3 5.4 copy-start.21
  455.5 94.2 %collective-permute-start.8 = (f32[2,256,768]{1,2,0:T(8,128)}, f32[2,256,768]{1,2,0:T(8,128)}, u32[]{:S(2)}, u32[]{:S(2)}) collective-permute-start(f32[2,256,768]{1,2,0:T(8,128)} %slice_select_fusion.2), channel_id=1, source_target_pairs={{0,16},{16,0},{8,24},{24,8},{32,48},{48,32},{40,56},{56,40},{64,80... | collective-permute-start | bytes 4718600 | tf_op jit(solution)/shard_map/ppermute | solution.py:18
  520.9 8.4 %copy-start.7 = (bf16[1,1024,768]{1,2,0:T(8,128)(2,1)S(1)}, bf16[1,1024,768]{1,2,0:T(8,128)(2,1)}, u32[]{:S(2)}) copy-start(bf16[1,1024,768]{1,2,0:T(8,128)(2,1)} %copy-done.6) | copy-start | bytes 4718596
  520.9 8.4 %copy-start.30 = (bf16[256,4,1024]{0,2,1:T(8,128)(2,1)S(1)}, bf16[256,4,1024]{0,2,1:T(8,128)(2,1)}, u32[]{:S(2)}) copy-start(bf16[256,4,1024]{0,2,1:T(8,128)(2,1)} %copy-done.29) | copy-start | bytes 6291460
  520.9 8.4 %copy-start.66 = (pred[256,4]{0,1:T(4,128)(4,1)S(1)}, pred[256,4]{0,1:T(4,128)(4,1)}, u32[]{:S(2)}) copy-start(pred[256,4]{0,1:T(4,128)(4,1)} %copy.247) | copy-start | bytes 3076
  522.3 7.5 %copy-start.34 = (bf16[256,4,1024]{0,2,1:T(8,128)(2,1)S(1)}, bf16[256,4,1024]{0,2,1:T(8,128)(2,1)}, u32[]{:S(2)}) copy-start(bf16[256,4,1024]{0,2,1:T(8,128)(2,1)} %copy-done.33) | copy-start | bytes 6291460
  522.3 7.5 %copy-start.53 = (f32[256,4,64]{0,2,1:T(8,128)S(1)}, f32[256,4,64]{0,2,1:T(8,128)}, u32[]{:S(2)}) copy-start(f32[256,4,64]{0,2,1:T(8,128)} %copy.153) | copy-start | bytes 786436
  522.3 7.5 %copy-start.67 = (pred[256,4]{0,1:T(4,128)(4,1)S(1)}, pred[256,4]{0,1:T(4,128)(4,1)}, u32[]{:S(2)}) copy-start(pred[256,4]{0,1:T(4,128)(4,1)} %copy.246) | copy-start | bytes 3076
  522.3 36.4 %collective-permute-start.6 = (f32[2,256,768]{1,2,0:T(8,128)}, f32[2,256,768]{1,2,0:T(8,128)}, u32[]{:S(2)}, u32[]{:S(2)}) collective-permute-start(f32[2,256,768]{1,2,0:T(8,128)} %slice_select_fusion.3), channel_id=1, source_target_pairs={{0,8},{8,0},{16,24},{24,16},{32,40},{40,32},{48,56},{56,48},{64,72... | collective-permute-start | bytes 4718600 | tf_op jit(solution)/shard_map/ppermute | solution.py:18
  529.8 19.8 %copy-start.5 = (f32[2,512,768]{1,2,0:T(8,128)S(1)}, f32[2,512,768]{1,2,0:T(8,128)}, u32[]{:S(2)}) copy-start(f32[2,512,768]{1,2,0:T(8,128)} %copy-done.4) | copy-start | bytes 9437188
  551.5 6.1 %copy-start.8 = (f32[2,256,768]{1,2,0:T(8,128)}, f32[2,256,768]{1,2,0:T(8,128)S(1)}, u32[]{:S(2)}) copy-start(f32[2,256,768]{1,2,0:T(8,128)S(1)} %select_add_fusion.2) | copy-start | bytes 4718596
  551.6 5.6 copy-start.32
  551.6 5.6 copy-start.54
  552.5 9.1 %collective-permute-start.9 = (f32[2,128,768]{1,2,0:T(8,128)}, f32[2,128,768]{1,2,0:T(8,128)}, u32[]{:S(2)}, u32[]{:S(2)}) collective-permute-start(f32[2,128,768]{1,2,0:T(8,128)} %slice_select_fusion.6), channel_id=1, source_target_pairs={{0,8},{8,0},{16,24},{24,16},{32,40},{40,32},{48,56},{56,48},{64,72... | collective-permute-start | bytes 2359304 | tf_op jit(solution)/shard_map/ppermute | solution.py:18
  570.2 3.9 copy-start.27
  570.2 3.9 copy-start.71
  570.2 3.9 copy-start.87
  571.6 7.4 %copy-start.1 = (bf16[1,256,768]{2,1,0:T(8,128)(2,1)S(1)}, bf16[1,256,768]{2,1,0:T(8,128)(2,1)}, u32[]{:S(2)}) copy-start(bf16[1,256,768]{2,1,0:T(8,128)(2,1)} %param.10) | copy-start | bytes 1179652
  (43 other events, 75.9 us)
Sparse Core Ops, SparseCore 0:
  10.1 43.7 all-gather.1
where the time goes:
time: 598 us; the launch traced here: 586 us
  waiting for transfers between devices  207 us (35%)
  local copies, waits for them, and re-layouts  132 us (22%)
  other arithmetic  121 us (20%)
  matrix products  67.9 us (11%)
  starting transfers between devices  41.3 us (7%)
  between operations  16.1 us (3%)
    ppermute x10, waiting for transfers between devices, swapped(): return lax.ppermute(block, axis, route)  184 us
    ppermute x10, starting transfers between devices, swapped(): return lax.ppermute(block, axis, route)  41.3 us
    broadcast_in_dim x26, local copies, waits for them, and re-layouts, spread_rows(): jnp.where(row_selector[None, :, :, None], vectors[:, None], 0.0)  26.6 us
    broadcast_in_dim x21, local copies, waits for them, and re-layouts, spread_stat(): jnp.where(row_selector[None], stat[:, None, :], fill_value)  26.4 us
    convert_element_type x6, other arithmetic, on_device(): probabilities = jnp.where(usable_rows, jnp.exp(attention_scores - branch_...  23.2 us
    all_gather x1, waiting for transfers between devices, on_device(): lax.all_gather(w_out, 'fsdp', axis=0, tiled=True)  22.6 us
    reduce_sum x6, other arithmetic, on_device(): jnp.sum(jnp.where(usable_rows, jnp.exp(attention_scores - branch_maximum[...  22.6 us
    dot_general x6, matrix products, on_device(): jnp.einsum('uhd,nhd->uhn', branch_parts[0][:, heads], key_groups[branch_i...  21.1 us
  transfers between devices with their start and end apart: 11, of which 7 were waited for; matrix products, arithmetic and copies ran while one was open for 16% of the time, Pallas kernels for 0%

commit v1 on v0

v1 whole, which is shorter than its diff:
```python
import jax
import jax.numpy as jnp
from jax import lax
from jax.experimental import pallas as pl
from jax.experimental.pallas import tpu as pltpu
from jax.sharding import PartitionSpec as P

HEADS = 12
HD = 64
GROUP = 8
ROWS = 256
HALF = 128
QUAD = GROUP // 2
SEG = GROUP * HALF
QB = 256
KC = 512
SUB = 256
NEG = -1e30
F32 = jnp.float32
BF16 = jnp.bfloat16
MESH = pl.DeviceIdType.MESH


def nt(a, b):
    return lax.dot_general(a, b, (((1,), (1,)), ((), ())), preferred_element_type=F32)


def nn(a, b):
    return jnp.dot(a, b, preferred_element_type=F32)


def row_perm(value):
    r = lax.broadcasted_iota(jnp.int32, (ROWS, ROWS), 0)
    c = lax.broadcasted_iota(jnp.int32, (ROWS, ROWS), 1)
    pos = jnp.where(r < HALF, 2 * r, 2 * r - (ROWS - 1))
    return jnp.where(c == pos, value, 0.0).astype(BF16)


def row_unperm():
    r = lax.broadcasted_iota(jnp.int32, (ROWS, ROWS), 1)
    c = lax.broadcasted_iota(jnp.int32, (ROWS, ROWS), 0)
    pos = jnp.where(r < HALF, 2 * r, 2 * r - (ROWS - 1))
    return jnp.where(c == pos, 1.0, 0.0).astype(BF16)


def kernel(
    q_ref, k_ref, v_ref, og_ref, w_ref, off_ref, valid_ref,
    dq_ref, dk_ref, dv_ref,
    qks, vds, qk, vd, kp, kt, w4, sbuf, dpbuf, dsp, acc, xsib, out, back, perm_og,
    w_send, w_recv, wf_send, wf_recv, a_send, a_recv, f_send, f_recv, x_send, x_recv, o_send, o_recv, l_sem,
):
    ctx = lax.axis_index("ctx")
    z = lax.axis_index("fsdp")
    nz = lax.axis_size("fsdp")
    m = ctx % GROUP
    base = ctx - m
    chip = m // 2
    core = m % 2
    half = m // QUAD
    valid = valid_ref[0]

    def dev(member):
        return (base + member, z)

    def remote(src, dst, ssem, rsem, to):
        return pltpu.make_async_remote_copy(
            src_ref=src, dst_ref=dst, send_sem=ssem, recv_sem=rsem, device_id=to, device_id_type=MESH
        )

    def full_head(p):
        return 3 * (p // 2) + 2 * (p % 2)

    barrier = pltpu.get_barrier_semaphore()
    for d in range(1, GROUP):
        pl.semaphore_signal(barrier, inc=1, device_id=dev(m ^ d), device_id_type=MESH)
    for d in range(1, nz):
        pl.semaphore_signal(barrier, inc=1, device_id=(ctx, (z + d) % nz), device_id_type=MESH)
    pl.semaphore_wait(barrier, GROUP - 1 + nz - 1)

    def w_copy(d):
        return remote(w_ref.at[core], w4.at[z, core], w_send.at[d], w_recv.at[d], (ctx, (z + d) % nz))

    def w_forward(d, c):
        frm = (z + nz - d) % nz
        return remote(w4.at[frm, c], w4.at[frm, c], wf_send.at[d], wf_recv.at[d], dev(m ^ 1))

    for d in range(1, nz):
        w_copy(d).start()
    own_w = pltpu.make_async_copy(w_ref.at[core], w4.at[z, core], l_sem.at[0])
    own_w.start()

    lane = lax.broadcasted_iota(jnp.int32, (HALF, 2 * HD), 1)
    low = lane < HD

    def takes_odd(tile):
        return jnp.where(low, off_ref[1, 2 * tile], off_ref[1, 2 * tile + 1]) == 1

    def pack(dst, left, right, tile):
        odd = takes_odd(tile)
        for s in range(2):
            a, b = (left[HALF:], left[:HALF]) if s == 0 else (left[:HALF], left[HALF:])
            l = jnp.where(odd, a, b)
            a, b = (right[HALF:], right[:HALF]) if s == 0 else (right[:HALF], right[HALF:])
            r = jnp.where(odd, a, b)
            dst[2 * tile, s] = jnp.where(low, l, pltpu.roll(r, HD, 1)).astype(BF16)
            dst[2 * tile + 1, s] = jnp.where(low, pltpu.roll(l, HD, 1), r).astype(BF16)

    def full_copy(src, dst, which, d):
        p = m ^ d
        return remote(
            src.at[full_head(p)], dst.at[0, :, m], a_send.at[which, 0, d], a_recv.at[which, 0, d], dev(p)
        )

    def shared_copy(src, dst, which, dx):
        to = chip ^ dx
        return remote(
            src.at[3 * to + 1], dst.at[1, :, m], a_send.at[which, 1, dx], a_recv.at[which, 1, m % QUAD],
            dev(2 * to + half),
        )

    def local_full(src, dst, which):
        return pltpu.make_async_copy(src.at[full_head(m)], dst.at[0, :, m], l_sem.at[1 + which])

    def local_shared(src, dst, which):
        return pltpu.make_async_copy(src.at[3 * chip + 1], dst.at[1, :, m], l_sem.at[3 + which])

    def exchange(src, dst, which):
        for d in range(1, GROUP):
            full_copy(src, dst, which, d).start()
        local_full(src, dst, which).start()
        for dx in range(1, QUAD):
            shared_copy(src, dst, which, dx).start()

        @pl.when(core != half)
        def _():
            shared_copy(src, dst, which, 0).start()

        @pl.when(core == half)
        def _():
            local_shared(src, dst, which).start()

    def wait_full(src, dst, which):
        local_full(src, dst, which).wait()
        for d in range(1, GROUP):
            remote(
                src.at[0], dst.at[0, :, m ^ d], a_send.at[which, 0, d], a_recv.at[which, 0, d], dev(m ^ d)
            ).wait_recv()

    def wait_shared(src, dst, which):
        for j in range(QUAD):
            s = QUAD * core + j

            @pl.when(s != m)
            def _():
                remote(
                    src.at[0], dst.at[1, :, s], a_send.at[which, 1, 0], a_recv.at[which, 1, j], dev(s)
                ).wait_recv()

        @pl.when(core == half)
        def _():
            local_shared(src, dst, which).wait()

    perm = row_perm(1.0)
    perm_q = row_perm(HD ** -0.5)
    for t in range(HEADS // 2):
        cols = slice(t * 128, (t + 1) * 128)
        pack(qks, nn(perm_q, q_ref[:, cols]), nn(perm, k_ref[:, cols]), t)
    exchange(qks, qk, 0)

    perm_og[...] = nn(perm, og_ref[...]).astype(BF16)

    for d in range(1, nz):
        frm = (z + nz - d) % nz
        remote(w_ref.at[core], w4.at[frm, core], w_send.at[d], w_recv.at[d], (ctx, frm)).wait_recv()
        w_forward(d, core).start()
    own_w.wait()
    w_forward(0, core).start()
    for d in range(nz):
        w_forward(d, 1 - core).wait_recv()
    grad = nt(perm_og[...], w4[...].reshape(HEADS * HD, HEADS * HD))
    r = lax.broadcasted_iota(jnp.int32, (ROWS, 1), 0)
    position = ctx * ROWS + jnp.where(r < HALF, 2 * r, 2 * r - (ROWS - 1))
    grad = jnp.where(position < valid, grad, 0.0)
    for t in range(HEADS // 2):
        cols = slice(t * 128, (t + 1) * 128)
        pack(vds, nn(perm, v_ref[:, cols]), grad[:, cols], t)
    exchange(vds, vd, 1)

    acc[...] = jnp.zeros_like(acc)

    def positions(row, cls, off):
        return base * ROWS + 2 * row + (off if cls == 0 else 1 - off)

    wide = lax.broadcasted_iota(jnp.int32, (KC, 2 * HD), 1)
    key_row = lax.broadcasted_iota(jnp.int32, (KC, 1), 0)

    def prepare(slot, cls, seg, off):
        bias = jnp.where(positions(seg * KC + key_row, cls, off) < valid, 0.0, NEG)
        x = qk[slot, cls, pl.ds(seg * QUAD, QUAD)].reshape(KC, 2 * HD).astype(F32)
        rows = pl.ds(pl.multiple_of(seg * KC, KC), KC)
        kp[slot, cls, rows] = jnp.where(wide >= HD, x, jnp.where(wide == 0, bias, 0.0)).astype(BF16)
        kt[slot, cls, :, rows] = jnp.transpose(x)[HD:].astype(BF16)

    qlane = lax.broadcasted_iota(jnp.int32, (QB, 2 * HD), 1)
    qlow = qlane < HD
    qrow = lax.broadcasted_iota(jnp.int32, (QB, 1), 0)

    def fold(x, op):
        return op(x.reshape(SUB // 8, 8, QB), axis=0)

    def block(slot, off, c, i):
        r0 = pl.multiple_of(c * KC + i * QB, QB)
        s0 = c * QUAD + 2 * i
        parts = []
        for cls in range(2):
            xq = qk[slot, cls, pl.ds(s0, 2)].reshape(QB, 2 * HD).astype(F32)
            xv = vd[slot, cls, pl.ds(s0, 2)].reshape(QB, 2 * HD).astype(F32)
            use = jnp.where(positions(r0 + qrow, cls, off) < valid, 1.0, 0.0)
            qp = jnp.where(qlow, jnp.where(qlane == 0, use, 0.0), pltpu.roll(xq, HD, 1)).astype(BF16)
            gp = jnp.where(qlow, 0.0, xv)
            g0 = gp.astype(BF16)
            gp = pltpu.roll(gp, HD, 1).astype(BF16)
            q0 = jnp.where(qlow, xq, 0.0).astype(BF16)
            grads = jnp.concatenate([q0, g0], axis=0)
            if cls == 0:
                chunks = [(0, c, 2), (0, 1 - c, 1), (1, c, 1)]
            else:
                chunks = [(0, c, 1), (1, c, 1)]
            subs = [(n, kc, seg, mult, u) for n, (kc, seg, mult) in enumerate(chunks) for u in range(KC // SUB)]
            top = jnp.full((8, QB), -jnp.inf, F32)
            for n, kc, seg, mult, u in subs:
                s = nt(kp[slot, kc, pl.ds(pl.multiple_of(seg * KC + u * SUB, SUB), SUB)], qp)
                sbuf[n, u * SUB:(u + 1) * SUB] = s
                top = jnp.maximum(top, fold(s, jnp.max))
            top = jnp.max(top, axis=0, keepdims=True)
            total = jnp.zeros((8, QB), F32)
            dot_sum = jnp.zeros((8, QB), F32)
            for n, kc, seg, mult, u in subs:
                su = slice(u * SUB, (u + 1) * SUB)
                per = SUB // HALF
                values = vd[slot, kc, pl.ds(seg * QUAD + u * per, per)].reshape(SUB, 2 * HD)
                dp = nt(values, gp)
                e = jnp.exp(sbuf[n, su] - top)
                sbuf[n, su] = e
                dpbuf[n, su] = dp
                total = total + mult * fold(e, jnp.sum)
                dot_sum = dot_sum + mult * fold(e * dp, jnp.sum)
            inv = 1.0 / jnp.sum(total, axis=0, keepdims=True)
            delta = jnp.sum(dot_sum, axis=0, keepdims=True) * inv
            dqt = jnp.zeros((HD, QB), F32)
            for n, (kc, seg, mult) in enumerate(chunks):
                rows = pl.ds(pl.multiple_of(seg * KC, KC), KC)
                for u in range(KC // SUB):
                    su = slice(u * SUB, (u + 1) * SUB)
                    p = sbuf[n, su] * inv
                    ds = p * (dpbuf[n, su] - delta)
                    dsp[cls, n, su, :QB] = ds.astype(BF16)
                    dsp[cls, n, su, QB:] = p.astype(BF16)
                acc[slot, kc, rows] += nn(dsp[cls, n], grads * mult if mult != 1 else grads)
                keys_t = kt[slot, kc, :, rows]
                dqt = dqt + nn(keys_t * mult if mult != 1 else keys_t, dsp[cls, n, :, :QB])
            parts.append(dqt)
        dq = jnp.transpose(jnp.concatenate(parts, axis=0)) * (HD ** -0.5)
        out[slot, pl.ds(s0, 2), 2] = dq.reshape(2, HALF, 2 * HD).astype(BF16)

    off0 = off_ref[1, full_head(m)]
    wait_full(qks, qk, 0)
    for cls in range(2):
        for seg in range(2):
            prepare(0, cls, seg, off0)
    wait_full(vds, vd, 1)

    @pl.loop(0, 4)
    def _(t):
        block(0, off0, t // 2, t % 2)

    for cls in range(2):
        out[0, :, cls] = acc[0, cls].reshape(GROUP, HALF, 2 * HD).astype(BF16)

    def out_full(d):
        p = m ^ d
        return remote(out.at[0, p], back.at[full_head(m)], o_send.at[0, d], o_recv.at[0, d], dev(p))

    for d in range(1, GROUP):
        out_full(d).start()
    own_full = pltpu.make_async_copy(out.at[0, m], back.at[full_head(m)], l_sem.at[5])
    own_full.start()

    off1 = off_ref[1, 3 * chip + 1]
    mine = pl.ds(QUAD * core, QUAD)
    theirs = pl.ds(QUAD * (1 - core), QUAD)

    def pass_on(dst, which, part):
        return remote(dst.at[1, 0, part], dst.at[1, 0, part], f_send.at[which], f_recv.at[which], dev(m ^ 1))

    for which, (src, dst) in enumerate(((qks, qk), (vds, vd))):
        wait_shared(src, dst, which)
        pass_on(dst, which, mine).start()
    for which, dst in enumerate((qk, vd)):
        pass_on(dst, which, theirs).wait_recv()
    prepare(1, 0, 0, off1)
    prepare(1, 0, 1, off1)
    prepare(1, 1, core, off1)

    @pl.loop(0, 2)
    def _(t):
        block(1, off1, core, t)

    def swap_terms(c):
        rows = pl.ds(pl.multiple_of(c * KC, KC), KC)
        return remote(acc.at[1, 0, rows], xsib, x_send.at[0], x_recv.at[0], dev(m ^ 1))

    swap_terms(1 - core).start()
    own_rows = pl.ds(pl.multiple_of(core * KC, KC), KC)
    out[1, mine, 1] = acc[1, 1, own_rows].reshape(QUAD, HALF, 2 * HD).astype(BF16)
    swap_terms(core).wait_recv()
    out[1, mine, 0] = (acc[1, 0, own_rows] + xsib[...]).reshape(QUAD, HALF, 2 * HD).astype(BF16)

    def out_shared(j):
        s = QUAD * core + j
        return remote(
            out.at[1, s], back.at[3 * chip + 1], o_send.at[1, j], o_recv.at[1, chip], dev(s)
        )

    own_shared = pltpu.make_async_copy(out.at[1, m], back.at[3 * chip + 1], l_sem.at[6])
    for j in range(QUAD):
        @pl.when(QUAD * core + j != m)
        def _():
            out_shared(j).start()

    @pl.when(core == half)
    def _():
        own_shared.start()

    own_full.wait()
    for d in range(1, GROUP):
        p = m ^ d
        remote(out.at[0, p], back.at[full_head(p)], o_send.at[0, d], o_recv.at[0, d], dev(p)).wait_recv()

    @pl.when(core == half)
    def _():
        own_shared.wait()

    for x in range(QUAD):
        @pl.when(2 * x + half != m)
        def _():
            remote(
                out.at[1, 0], back.at[3 * x + 1], o_send.at[1, 0], o_recv.at[1, x], dev(2 * x + half)
            ).wait_recv()

    unperm = row_unperm()
    for t in range(HEADS // 2):
        cols = slice(t * 128, (t + 1) * 128)
        odd = takes_odd(t)

        def put(ref, sel, oth):
            rows = jnp.concatenate([jnp.where(odd, oth, sel), jnp.where(odd, sel, oth)], axis=0)
            ref[:, cols] = nn(unperm, rows.astype(BF16)).astype(BF16)

        first = [back[2 * t, n].astype(F32) for n in range(3)]
        second = [back[2 * t + 1, n].astype(F32) for n in range(3)]
        left = [jnp.where(low, first[n], pltpu.roll(second[n], HD, 1)) for n in range(3)]
        right = [jnp.where(low, pltpu.roll(first[n], HD, 1), second[n]) for n in range(3)]
        put(dk_ref, left[0], left[1])
        put(dv_ref, right[0], right[1])
        put(dq_ref, left[2], right[2])

    for d in range(1, nz):
        w_copy(d).wait_send()
    for d in range(nz):
        w_forward(d, core).wait_send()
    for which, (src, dst) in enumerate(((qks, qk), (vds, vd))):
        for d in range(1, GROUP):
            full_copy(src, dst, which, d).wait_send()
        for dx in range(1, QUAD):
            shared_copy(src, dst, which, dx).wait_send()

        @pl.when(core != half)
        def _():
            shared_copy(src, dst, which, 0).wait_send()
        pass_on(dst, which, mine).wait_send()
    for d in range(1, GROUP):
        out_full(d).wait_send()
    swap_terms(1 - core).wait_send()
    for j in range(QUAD):
        @pl.when(QUAD * core + j != m)
        def _():
            out_shared(j).wait_send()


def on_device(query_in, key_in, value_in, out_grad, w_out, head_offsets, valid_tiles):
    width = HEADS * HD
    nz = lax.axis_size("fsdp")
    w_rows = w_out.shape[0] // 2
    spec = jax.ShapeDtypeStruct((ROWS, width), BF16)
    vmem = pl.BlockSpec(memory_space=pltpu.VMEM)
    smem = pl.BlockSpec(memory_space=pltpu.SMEM)
    dma = pltpu.SemaphoreType.DMA
    outs = pl.pallas_call(
        kernel,
        out_shape=[spec] * 3,
        in_specs=[vmem] * 5 + [smem] * 2,
        out_specs=[vmem] * 3,
        scratch_shapes=[
            pltpu.VMEM((HEADS, 2, HALF, 2 * HD), BF16),
            pltpu.VMEM((HEADS, 2, HALF, 2 * HD), BF16),
            pltpu.VMEM((2, 2, GROUP, HALF, 2 * HD), BF16),
            pltpu.VMEM((2, 2, GROUP, HALF, 2 * HD), BF16),
            pltpu.VMEM((2, 2, SEG, 2 * HD), BF16),
            pltpu.VMEM((2, 2, HD, SEG), BF16),
            pltpu.VMEM((nz, 2, w_rows, width), BF16),
            pltpu.VMEM((3, KC, QB), F32),
            pltpu.VMEM((3, KC, QB), F32),
            pltpu.VMEM((2, 3, KC, 2 * QB), BF16),
            pltpu.VMEM((2, 2, SEG, 2 * HD), F32),
            pltpu.VMEM((KC, 2 * HD), F32),
            pltpu.VMEM((2, GROUP, 3, HALF, 2 * HD), BF16),
            pltpu.VMEM((HEADS, 3, HALF, 2 * HD), BF16),
            pltpu.VMEM((ROWS, width), BF16),
            dma((nz,)), dma((nz,)), dma((nz,)), dma((nz,)),
            dma((2, 2, GROUP)), dma((2, 2, GROUP)),
            dma((2,)), dma((2,)), dma((1,)), dma((1,)),
            dma((2, GROUP)), dma((2, GROUP)), dma((7,)),
        ],
        compiler_params=pltpu.CompilerParams(
            collective_id=0, has_side_effects=True, vmem_limit_bytes=56 * 1024 * 1024
        ),
        cost_estimate=pl.CostEstimate(flops=4_000_000_000, bytes_accessed=3_000_000, transcendentals=4_000_000),
    )(
        query_in[0], key_in[0], value_in[0], out_grad[0],
        w_out.reshape(2, w_rows, width), head_offsets, valid_tiles,
    )
    return tuple(o[None] for o in outs)


def solution(mesh):
    rows = P("fsdp", "ctx", None)
    return jax.shard_map(
        on_device,
        mesh=mesh,
        in_specs=(rows, rows, rows, rows, P("fsdp", None), P(), P("fsdp")),
        out_specs=(rows, rows, rows),
        check_vma=False,
    )
```

time: 598 us -> 74.9 us (0.13); the launches traced: 586 us -> 74.6 us
  waiting for transfers between devices: 207 us -> 0 us
  local copies, waits for them, and re-layouts: 132 us -> 3.7 us
  other arithmetic: 121 us -> 0 us
  Pallas kernels: 0 us -> 69.6 us
  matrix products: 67.9 us -> 0 us
  starting transfers between devices: 41.3 us -> 0 us
  between operations: 16.1 us -> 1.3 us
    ppermute x10 -> x0, waiting for transfers between devices: 184 us -> none  [swapped(): return lax.ppermute(block, axis, route)]
    pallas_call x0 -> x1, Pallas kernels: none -> 69.6 us  [on_device(): pl.pallas_call(kernel, out_shape=[spec] * 3, in_specs=[vmem] * 5 + [smem]...]
    dot_general x37 -> x0, matrix products: 67.9 us -> none  [the longest x6 21.1 us: on_device(): jnp.einsum('uhd,nhd->uhn', branch_parts[0][:, heads], key_groups[branch_i...]
    broadcast_in_dim x47 -> x0, local copies, waits for them, and re-layouts: 53 us -> none  [the longest x26 26.6 us: spread_rows(): jnp.where(row_selector[None, :, :, None], vectors[:, None], 0.0)]
    ppermute x10 -> x0, starting transfers between devices: 41.3 us -> none  [swapped(): return lax.ppermute(block, axis, route)]
    reduce_sum x15 -> x0, other arithmetic: 36.4 us -> none  [the longest x6 22.6 us: on_device(): jnp.sum(jnp.where(usable_rows, jnp.exp(attention_scores - branch_maximum[...]
    convert_element_type x8 -> x0, other arithmetic: 28.3 us -> none  [the longest x6 23.2 us: on_device(): probabilities = jnp.where(usable_rows, jnp.exp(attention_scores - branch_...]
    reduce_sum x18 -> x0, local copies, waits for them, and re-layouts: 26.5 us -> none  [the longest x9 13.5 us: pick_stat(): return jnp.sum(jnp.where(row_selector[None], reshaped_rows, 0.0), axis=1)]
  transfers between devices with their start and end apart: 11 -> 0, of which waited for: 7 -> 0; matrix products, arithmetic and copies ran while one was open for 16% -> 0% of each run, Pallas kernels for 0% -> 0%
where the time goes in v1:
time: 74.9 us; the launch traced here: 74.6 us
  Pallas kernels  69.6 us (93%)
  local copies, waits for them, and re-layouts  3.7 us (5%)
  between operations  1.3 us (2%)
    pallas_call x1, Pallas kernels, on_device(): pl.pallas_call(kernel, out_shape=[spec] * 3, in_specs=[vmem] * 5 + [smem]...  69.6 us
    unnamed x7, local copies, waits for them, and re-layouts  3.7 us

profile of v1, /device:TPU:1, one launch (start us, length us, event | category | flops | bytes accessed | tf_op | source)
XLA Modules:
  0.0 74.6 jit_solution(15526417664909400588)
XLA Ops:
  1.3 69.6 %shard_map.94 = (bf16[256,768]{1,0:T(8,128)(2,1)}, bf16[256,768]{1,0:T(8,128)(2,1)}, bf16[256,768]{1,0:T(8,128)(2,1)}) custom-call(bf16[256,768]{1,0:T(8,128)(2,1)} %bitcast.11, bf16[256,768]{1,0:T(8,128)(2,1)} %bitcast.12, bf16[256,768]{1,0:T(8,128)(2,1)} %bitcast.13, bf16[256,768]{1,0:T(8,128)(2,1)} %bitcast.14, bf16[2,48,768]{2,1,0:T(8,128)(2,1)} %bitcast.15, ...), custom_call_target="tpu_custom_call" | custom-call | flops 4000000000 | bytes 3000000 | tf_op jit(solution)/shard_map/pallas_call | solution.py:399
  70.9 0.0 copy-start.1
  70.9 1.8 %copy.14 = bf16[1,256,768]{2,1,0:T(8,128)(2,1)} copy(bf16[1,256,768]{2,1,0:T(8,128)(2,1)} %bitcast.10) | data formatting | bytes 786432
  72.8 0.0 copy-done.1
  72.8 0.0 copy-start
  72.8 0.7 copy.15
  73.5 0.4 copy-done
  73.9 0.7 copy.16
Async XLA Ops:
  70.9 1.8 %copy-start.1 = (bf16[256,768]{1,0:T(8,128)(2,1)S(1)}, bf16[256,768]{1,0:T(8,128)(2,1)}, u32[]{:S(2)}) copy-start(bf16[256,768]{1,0:T(8,128)(2,1)} %get-tuple-element.7) | copy-start | bytes 1179652
  72.8 1.1 %copy-start = (bf16[256,768]{1,0:T(8,128)(2,1)S(1)}, bf16[256,768]{1,0:T(8,128)(2,1)}, u32[]{:S(2)}) copy-start(bf16[256,768]{1,0:T(8,128)(2,1)} %get-tuple-element.8) | copy-start | bytes 1179652

commit v2 on v1

v2 whole, which is shorter than its diff:
```python
import jax
import jax.numpy as jnp
from jax import lax
from jax.experimental import pallas as pl
from jax.experimental.pallas import tpu as pltpu
from jax.sharding import PartitionSpec as P

HEADS = 12
HD = 64
GROUP = 8
ROWS = 256
HALF = 128
QUAD = GROUP // 2
SEG = GROUP * HALF
QB = 256
KC = 512
SUB = 256
NEG = -1e30
PAIRS = 3
EARLY = 2
W_CUT = 32
BLOCKS = 6
F32 = jnp.float32
BF16 = jnp.bfloat16
MESH = pl.DeviceIdType.MESH


def nt(a, b):
    return lax.dot_general(a, b, (((1,), (1,)), ((), ())), preferred_element_type=F32)


def nn(a, b):
    return jnp.dot(a, b, preferred_element_type=F32)


def row_perm(value):
    r = lax.broadcasted_iota(jnp.int32, (ROWS, ROWS), 0)
    c = lax.broadcasted_iota(jnp.int32, (ROWS, ROWS), 1)
    pos = jnp.where(r < HALF, 2 * r, 2 * r - (ROWS - 1))
    return jnp.where(c == pos, value, 0.0).astype(BF16)


def row_unperm():
    r = lax.broadcasted_iota(jnp.int32, (ROWS, ROWS), 1)
    c = lax.broadcasted_iota(jnp.int32, (ROWS, ROWS), 0)
    pos = jnp.where(r < HALF, 2 * r, 2 * r - (ROWS - 1))
    return jnp.where(c == pos, 1.0, 0.0).astype(BF16)


def kernel(
    q_in, k_in, v_in, og_in, w_ref, off_ref, valid_ref,
    back,
    xin, qks, vs, gs, qk, vin, gin, vd, kp, kt, w4, ebuf, stat, dpbuf, dsp, acc, xsib, out, dqbuf, og_perm,
    w_send, w_recv, a_send, a_recv, f_send, f_recv, x_send, x_recv, o_send, o_recv,
    l_sem, in_sem,
):
    ctx = lax.axis_index("ctx")
    z = lax.axis_index("fsdp")
    nz = lax.axis_size("fsdp")
    m = ctx % GROUP
    base = ctx - m
    chip = m // 2
    core = m % 2
    half = m // QUAD
    valid = valid_ref[0]

    def dev(member):
        return (base + member, z)

    def remote(src, dst, ssem, rsem, to):
        return pltpu.make_async_remote_copy(
            src_ref=src, dst_ref=dst, send_sem=ssem, recv_sem=rsem, device_id=to, device_id_type=MESH
        )

    def full_head(p):
        return 3 * (p // 2) + 2 * (p % 2)

    barrier = pltpu.get_barrier_semaphore()
    for d in range(1, GROUP):
        pl.semaphore_signal(barrier, inc=1, device_id=dev(m ^ d), device_id_type=MESH)
    for d in (1, 2, nz - 2, nz - 1):
        pl.semaphore_signal(barrier, inc=1, device_id=(ctx, (z + d) % nz), device_id_type=MESH)
    loads = [pltpu.make_async_copy(x, xin.at[n], in_sem.at[n]) for n, x in enumerate((q_in, k_in, v_in, og_in))]
    for c in loads:
        c.start()
    own_w = pltpu.make_async_copy(w_ref, w4.at[z], l_sem.at[0])
    own_w.start()

    turn = 1 - 2 * core
    pieces = (pl.ds(0, W_CUT), pl.ds(W_CUT, w_ref.shape[1] - W_CUT))

    def w_copy(way, step, n, sender):
        by = turn if way == 0 else -turn
        hop = 2 if step == 4 else 1
        frm = (z - (step - hop if sender else step) * by + nz) % nz
        rows = pieces[n]
        src = w_ref.at[core, rows] if step == 1 else w4.at[frm, core, rows]
        return frm, remote(
            src, w4.at[frm, core, rows], w_send.at[0],
            w_recv.at[(way * 4 + step - 1) * 2 + n], (ctx, (z + hop * by + nz) % nz),
        )

    def arrived(ref, sem):
        pltpu.make_async_copy(ref, ref, sem).wait()

    def w_forward(frm, c):
        return remote(w4.at[frm, c], w4.at[frm, c], w_send.at[1], w_recv.at[16], dev(m ^ 1))

    lane = lax.broadcasted_iota(jnp.int32, (HALF, 2 * HD), 1)
    low = lane < HD

    def takes_odd(tile):
        return jnp.where(low, off_ref[1, 2 * tile], off_ref[1, 2 * tile + 1]) == 1

    def classes(x, odd):
        return jnp.where(odd, x[HALF:], x[:HALF]), jnp.where(odd, x[:HALF], x[HALF:])

    def side_by_side(l, r):
        one = jnp.where(low, l, pltpu.roll(r, HD, 1)).astype(BF16)
        return one, jnp.where(low, pltpu.roll(l, HD, 1), r).astype(BF16)

    def pack_pair(dst, left, right, tile):
        odd = takes_odd(tile)
        for cls, (l, r) in enumerate(zip(classes(left, odd), classes(right, odd))):
            dst[2 * tile, cls], dst[2 * tile + 1, cls] = side_by_side(l, r)

    def pack_one(dst, x, tile):
        dst[2 * tile], dst[2 * tile + 1] = side_by_side(*classes(x, takes_odd(tile)))

    def place(dst, slot, s):
        return dst.at[slot, :, s] if len(dst.shape) == 5 else dst.at[slot, s]

    def full_copy(src, dst, which, d):
        p = m ^ d
        return remote(
            src.at[full_head(p)], place(dst, 0, m), a_send.at[which], a_recv.at[which, 0], dev(p)
        )

    def shared_copy(src, dst, which, dx):
        to = chip ^ dx
        return remote(
            src.at[3 * to + 1], place(dst, 1, m), a_send.at[which], a_recv.at[which, 1],
            dev(2 * to + half),
        )

    def local_full(src, dst, which):
        return pltpu.make_async_copy(src.at[full_head(m)], place(dst, 0, m), a_recv.at[which, 0])

    def local_shared(src, dst, which):
        return pltpu.make_async_copy(src.at[3 * chip + 1], place(dst, 1, m), a_recv.at[which, 1])

    def exchange(src, dst, which):
        for d in range(1, GROUP):
            full_copy(src, dst, which, d).start()
        local_full(src, dst, which).start()
        for dx in range(1, QUAD):
            shared_copy(src, dst, which, dx).start()

        @pl.when(core != half)
        def _():
            shared_copy(src, dst, which, 0).start()

        @pl.when(core == half)
        def _():
            local_shared(src, dst, which).start()

    def wait_full(dst, which):
        arrived(dst.at[0], a_recv.at[which, 0])

    def wait_shared(dst, which):
        part = pl.ds(QUAD * core, QUAD)
        arrived(dst.at[1, :, part] if which == 0 else dst.at[1, part], a_recv.at[which, 1])

    def positions(row, cls, off):
        return base * ROWS + 2 * row + (off if cls == 0 else 1 - off)

    wide = lax.broadcasted_iota(jnp.int32, (KC, 2 * HD), 1)
    key_row = lax.broadcasted_iota(jnp.int32, (KC, 1), 0)

    def prepare(slot, cls, seg, off):
        bias = jnp.where(positions(seg * KC + key_row, cls, off) < valid, 0.0, NEG)
        x = qk[slot, cls, pl.ds(seg * QUAD, QUAD)].reshape(KC, 2 * HD).astype(F32)
        rows = pl.ds(pl.multiple_of(seg * KC, KC), KC)
        kp[slot, cls, rows] = jnp.where(wide >= HD, x, jnp.where(wide == 0, bias, 0.0)).astype(BF16)
        kt[slot, cls, :, rows] = jnp.transpose(x)[HD:].astype(BF16)

    def join(slot, cls, seg, with_grad):
        part = pl.ds(seg * QUAD, QUAD)
        x = vin[slot, part].reshape(KC, 2 * HD).astype(F32)
        g = 0.0
        if cls:
            x = pltpu.roll(x, HD, 1)
        if with_grad:
            g = gin[slot, part].reshape(KC, 2 * HD).astype(F32)
            if not cls:
                g = pltpu.roll(g, HD, 1)
        vd[slot, cls, part] = jnp.where(wide < HD, x, g).astype(BF16).reshape(QUAD, HALF, 2 * HD)

    qlane = lax.broadcasted_iota(jnp.int32, (QB, 2 * HD), 1)
    qlow = qlane < HD
    qrow = lax.broadcasted_iota(jnp.int32, (QB, 1), 0)

    def fold(x, op):
        return op(x.reshape(SUB // 8, 8, QB), axis=0)

    def chunks_of(c, cls):
        if cls == 0:
            return [(0, 0, c, 2), (1, 0, 1 - c, 1), (2, 1, c, 1)]
        return [(3, 0, c, 1), (4, 1, c, 1)]

    def scores(slot, off, c, i, cls):
        b = 4 * slot + (2 * c + i if slot == 0 else i)
        r0 = pl.multiple_of(c * KC + i * QB, QB)
        xq = qk[slot, cls, pl.ds(c * QUAD + 2 * i, 2)].reshape(QB, 2 * HD).astype(F32)
        use = jnp.where(positions(r0 + qrow, cls, off) < valid, 1.0, 0.0)
        qp = jnp.where(qlow, jnp.where(qlane == 0, use, 0.0), pltpu.roll(xq, HD, 1)).astype(BF16)
        chunks = chunks_of(c, cls)
        top = jnp.full((8, QB), -jnp.inf, F32)
        for n, kc, seg, mult in chunks:
            for u in range(KC // SUB):
                s = nt(kp[slot, kc, pl.ds(pl.multiple_of(seg * KC + u * SUB, SUB), SUB)], qp)
                ebuf[b, n, u * SUB:(u + 1) * SUB] = s
                top = jnp.maximum(top, fold(s, jnp.max))
        top = jnp.max(top, axis=0, keepdims=True)
        total = jnp.zeros((8, QB), F32)
        for n, kc, seg, mult in chunks:
            for u in range(KC // SUB):
                su = slice(u * SUB, (u + 1) * SUB)
                e = jnp.exp(ebuf[b, n, su] - top)
                ebuf[b, n, su] = e
                total = total + mult * fold(e, jnp.sum)
        stat[b, cls] = 1.0 / jnp.sum(total, axis=0, keepdims=True)

    def gradients(slot, c, i, cls):
        b = 4 * slot + (2 * c + i if slot == 0 else i)
        s0 = c * QUAD + 2 * i
        xq = qk[slot, cls, pl.ds(s0, 2)].reshape(QB, 2 * HD).astype(F32)
        xv = vd[slot, cls, pl.ds(s0, 2)].reshape(QB, 2 * HD).astype(F32)
        gp = jnp.where(qlow, 0.0, xv)
        g0 = gp.astype(BF16)
        gp = pltpu.roll(gp, HD, 1).astype(BF16)
        q0 = jnp.where(qlow, xq, 0.0).astype(BF16)
        grads = jnp.concatenate([q0, g0], axis=0)
        chunks = chunks_of(c, cls)
        dot_sum = jnp.zeros((8, QB), F32)
        for n, kc, seg, mult in chunks:
            for u in range(KC // SUB):
                su = slice(u * SUB, (u + 1) * SUB)
                per = SUB // HALF
                values = vd[slot, kc, pl.ds(seg * QUAD + u * per, per)].reshape(SUB, 2 * HD)
                dp = nt(values, gp)
                dpbuf[n, su] = dp
                dot_sum = dot_sum + mult * fold(ebuf[b, n, su] * dp, jnp.sum)
        inv = stat[b, cls]
        delta = jnp.sum(dot_sum, axis=0, keepdims=True) * inv
        dqt = jnp.zeros((HD, QB), F32)
        for n, kc, seg, mult in chunks:
            rows = pl.ds(pl.multiple_of(seg * KC, KC), KC)
            for u in range(KC // SUB):
                su = slice(u * SUB, (u + 1) * SUB)
                p = ebuf[b, n, su] * inv
                ds = p * (dpbuf[n, su] - delta)
                dsp[n, su, :QB] = ds.astype(BF16)
                dsp[n, su, QB:] = p.astype(BF16)
            acc[slot, kc, rows] += nn(dsp[n], grads * mult if mult != 1 else grads)
            keys_t = kt[slot, kc, :, rows]
            dqt = dqt + nn(keys_t * mult if mult != 1 else keys_t, dsp[n, :, :QB])
        return dqt

    def put_dq(slot, s0, sel, oth):
        dq = jnp.transpose(jnp.concatenate([sel, oth], axis=0)) * (HD ** -0.5)
        out[slot, pl.ds(s0, 2), 2] = dq.reshape(2, HALF, 2 * HD).astype(BF16)

    def send_out(slot, s, kind):
        head = full_head(m) if slot == 0 else 3 * chip + 1
        return remote(
            out.at[slot, s, kind], back.at[head, kind], o_send.at[0], o_recv.at[0], dev(s)
        )

    def keep_out(slot, kind):
        head = full_head(m) if slot == 0 else 3 * chip + 1
        return pltpu.make_async_copy(out.at[slot, m, kind], back.at[head, kind], o_recv.at[0])

    def start_out(slot, s, kind):
        @pl.when(s != m)
        def _():
            send_out(slot, s, kind).start()

        @pl.when(s == m)
        def _():
            keep_out(slot, kind).start()

    mine = pl.ds(QUAD * core, QUAD)
    theirs = pl.ds(QUAD * (1 - core), QUAD)

    def pass_on(dst, which, part):
        ref = dst.at[1, 0, part] if which == 0 else dst.at[1, part]
        return remote(ref, ref, f_send.at[which], f_recv.at[which], dev(m ^ 1))

    off0 = off_ref[1, full_head(m)]
    off1 = off_ref[1, 3 * chip + 1]

    perm = row_perm(1.0)
    perm_q = row_perm(HD ** -0.5)
    loads[0].wait()
    loads[1].wait()
    for t in range(HEADS // 2):
        cols = slice(t * 128, (t + 1) * 128)
        pack_pair(qks, nn(perm_q, xin[0, :, cols]), nn(perm, xin[1, :, cols]), t)
    pl.semaphore_wait(barrier, GROUP - 1 + 4)
    for n in range(2):
        for way in range(2):
            w_copy(way, 1, n, True)[1].start()
    exchange(qks, qk, 0)

    loads[2].wait()
    for t in range(HEADS // 2):
        pack_one(vs, nn(perm, xin[2, :, t * 128:(t + 1) * 128]), t)
    exchange(vs, vin, 1)

    loads[3].wait()
    og_perm[...] = nn(perm, xin[3]).astype(BF16)
    acc[...] = jnp.zeros_like(acc)
    for step in range(1, 4):
        for n in range(2):
            for way in range(2):
                frm, arrival = w_copy(way, step, n, False)
                arrival.wait_recv()
                if step < 3:
                    w_copy(way, step + 1, n, True)[1].start()
                if step == 2 and n == way:
                    w_copy(way, 4, n, True)[1].start()
                if n == 1:
                    w_forward(frm, core).start()

    wait_full(qk, 0)
    for cls in range(2):
        for seg in range(2):
            prepare(0, cls, seg, off0)

    @pl.loop(0, EARLY)
    def _(t):
        for cls in range(2):
            scores(0, off0, t // 2, t % 2, cls)

    for way in range(2):
        frm, arrival = w_copy(way, 4, way, False)
        arrival.wait_recv()
    w_forward(frm, core).start()
    own_w.wait()
    arrived(w4.at[pl.ds(0, nz - 1), 0], w_recv.at[16])
    grad = nt(og_perm[...], w4[...].reshape(HEADS * HD, HEADS * HD))
    r = lax.broadcasted_iota(jnp.int32, (ROWS, 1), 0)
    position = ctx * ROWS + jnp.where(r < HALF, 2 * r, 2 * r - (ROWS - 1))
    grad = jnp.where(position < valid, grad, 0.0)
    for t in range(HEADS // 2):
        cols = slice(t * 128, (t + 1) * 128)
        pack_one(gs, grad[:, cols], t)
    exchange(gs, gin, 2)

    wait_shared(qk, 0)
    pass_on(qk, 0, mine).start()

    @pl.loop(EARLY, 4)
    def _(t):
        for cls in range(2):
            scores(0, off0, t // 2, t % 2, cls)

    pass_on(qk, 0, theirs).wait_recv()
    prepare(1, 0, 0, off1)
    prepare(1, 0, 1, off1)
    prepare(1, 1, core, off1)

    @pl.loop(0, 2)
    def _(t):
        for cls in range(2):
            scores(1, off1, core, t, cls)

    def segment(slot, c, middle):
        @pl.loop(0, 2)
        def _(i):
            dqbuf[i] = gradients(slot, c, i, 0)

        middle()

        @pl.loop(0, 2)
        def _(i):
            s0 = QUAD * c + 2 * i
            put_dq(slot, s0, dqbuf[i], gradients(slot, c, i, 1))
            for e in range(2):
                start_out(slot, s0 + e, 2)

    def send_terms(slot, cls, c, extra=None):
        x = acc[slot, cls, pl.ds(pl.multiple_of(c * KC, KC), KC)]
        if extra is not None:
            x = x + extra
        out[slot, pl.ds(QUAD * c, QUAD), cls] = x.reshape(QUAD, HALF, 2 * HD).astype(BF16)
        for j in range(QUAD):
            start_out(slot, QUAD * c + j, cls)

    def swap_terms(c):
        rows = pl.ds(pl.multiple_of(c * KC, KC), KC)
        return remote(acc.at[1, 0, rows], xsib, x_send.at[0], x_recv.at[0], dev(m ^ 1))

    wait_shared(vin, 1)
    pass_on(vin, 1, mine).start()
    wait_shared(gin, 2)
    join(1, 0, core, True)
    join(1, 1, core, True)
    pass_on(vin, 1, theirs).wait_recv()
    join(1, 0, 1 - core, False)
    segment(1, core, lambda: swap_terms(1 - core).start())
    send_terms(1, 1, core)
    swap_terms(core).wait_recv()
    send_terms(1, 0, core, xsib[...])

    wait_full(vin, 1)
    wait_full(gin, 2)
    for cls in range(2):
        for c in range(2):
            join(0, cls, c, True)
    segment(0, core, lambda: None)
    send_terms(0, 1, core)
    segment(0, 1 - core, lambda: send_terms(0, 0, core))
    send_terms(0, 1, 1 - core)
    send_terms(0, 0, 1 - core)

    arrived(back, o_recv.at[0])

    arrived(w4.at[pl.ds(0, nz - 1), 0], w_send.at[0])
    arrived(w4.at[pl.ds(0, nz - 1), 0], w_send.at[1])
    swap_terms(1 - core).wait_send()
    pass_on(qk, 0, mine).wait_send()
    pass_on(vin, 1, mine).wait_send()

    def all_left(blocks):
        for which, src in enumerate((qks, vs, gs)):
            arrived(src.at[pl.ds(0, blocks)], a_send.at[which])
        arrived(back.at[pl.ds(0, blocks)], o_send.at[0])

    @pl.when(core != half)
    def _():
        all_left(GROUP - 1 + QUAD)

    @pl.when(core == half)
    def _():
        all_left(GROUP - 1 + QUAD - 1)


def finish(off_ref, back, dq_ref, dk_ref, dv_ref):
    lane = lax.broadcasted_iota(jnp.int32, (HALF, 2 * HD), 1)
    low = lane < HD
    unperm = row_unperm()
    first = pl.program_id(0) * PAIRS
    for t in range(PAIRS):
        cols = slice(t * 128, (t + 1) * 128)
        odd = jnp.where(low, off_ref[1, 2 * (first + t)], off_ref[1, 2 * (first + t) + 1]) == 1

        def put(ref, sel, oth):
            rows = jnp.concatenate([jnp.where(odd, oth, sel), jnp.where(odd, sel, oth)], axis=0)
            ref[:, cols] = nn(unperm, rows.astype(BF16)).astype(BF16)

        one = [back[2 * t, n].astype(F32) for n in range(3)]
        two = [back[2 * t + 1, n].astype(F32) for n in range(3)]
        left = [jnp.where(low, one[n], pltpu.roll(two[n], HD, 1)) for n in range(3)]
        right = [jnp.where(low, pltpu.roll(one[n], HD, 1), two[n]) for n in range(3)]
        put(dk_ref, left[0], left[1])
        put(dv_ref, right[0], right[1])
        put(dq_ref, left[2], right[2])


def on_device(query_in, key_in, value_in, out_grad, w_out, head_offsets, valid_tiles):
    width = HEADS * HD
    nz = lax.axis_size("fsdp")
    w_rows = w_out.shape[0] // 2
    far = pl.BlockSpec(memory_space=pl.ANY)
    smem = pl.BlockSpec(memory_space=pltpu.SMEM)
    dma = pltpu.SemaphoreType.DMA
    back = pl.pallas_call(
        kernel,
        out_shape=jax.ShapeDtypeStruct((HEADS, 3, HALF, 2 * HD), BF16),
        in_specs=[far] * 5 + [smem] * 2,
        out_specs=far,
        scratch_shapes=[
            pltpu.VMEM((4, ROWS, width), BF16),
            pltpu.VMEM((HEADS, 2, HALF, 2 * HD), BF16),
            pltpu.VMEM((HEADS, HALF, 2 * HD), BF16),
            pltpu.VMEM((HEADS, HALF, 2 * HD), BF16),
            pltpu.VMEM((2, 2, GROUP, HALF, 2 * HD), BF16),
            pltpu.VMEM((2, GROUP, HALF, 2 * HD), BF16),
            pltpu.VMEM((2, GROUP, HALF, 2 * HD), BF16),
            pltpu.VMEM((2, 2, GROUP, HALF, 2 * HD), BF16),
            pltpu.VMEM((2, 2, SEG, 2 * HD), BF16),
            pltpu.VMEM((2, 2, HD, SEG), BF16),
            pltpu.VMEM((nz, 2, w_rows, width), BF16),
            pltpu.VMEM((BLOCKS, 5, KC, QB), F32),
            pltpu.VMEM((BLOCKS, 2, 1, QB), F32),
            pltpu.VMEM((5, KC, QB), F32),
            pltpu.VMEM((5, KC, 2 * QB), BF16),
            pltpu.VMEM((2, 2, SEG, 2 * HD), F32),
            pltpu.VMEM((KC, 2 * HD), F32),
            pltpu.VMEM((2, GROUP, 3, HALF, 2 * HD), BF16),
            pltpu.VMEM((2, HD, QB), F32),
            pltpu.VMEM((ROWS, width), BF16),
            dma((2,)), dma((17,)), dma((3,)), dma((3, 2)),
            dma((2,)), dma((2,)), dma((1,)), dma((1,)), dma((1,)), dma((1,)), dma((1,)), dma((4,)),
        ],
        compiler_params=pltpu.CompilerParams(
            collective_id=0, has_side_effects=True, vmem_limit_bytes=56 * 1024 * 1024
        ),
        cost_estimate=pl.CostEstimate(flops=4_000_000_000, bytes_accessed=3_000_000, transcendentals=4_000_000),
    )(
        query_in[0], key_in[0], value_in[0], out_grad[0],
        w_out.reshape(2, w_rows, width), head_offsets, valid_tiles,
    )
    columns = pl.BlockSpec((ROWS, PAIRS * 2 * HD), lambda t: (0, t))
    outs = pl.pallas_call(
        finish,
        grid=(HEADS // 2 // PAIRS,),
        out_shape=[jax.ShapeDtypeStruct((ROWS, width), BF16)] * 3,
        in_specs=[smem, pl.BlockSpec((2 * PAIRS, 3, HALF, 2 * HD), lambda t: (t, 0, 0, 0))],
        out_specs=[columns] * 3,
    )(head_offsets, back)
    return tuple(o[None] for o in outs)


def solution(mesh):
    rows = P("fsdp", "ctx", None)
    return jax.shard_map(
        on_device,
        mesh=mesh,
        in_specs=(rows, rows, rows, rows, P("fsdp", None), P(), P("fsdp")),
        out_specs=(rows, rows, rows),
        check_vma=False,
    )
```

time: 74.9 us -> 61.1 us (0.82)
  Pallas kernels: 69.6 us -> 59.7 us
  local copies, waits for them, and re-layouts: 3.7 us -> 0 us
    pallas_call x1 -> x2, Pallas kernels: 69.6 us -> 59.7 us  [the longest x1 56.6 us: on_device(): pl.pallas_call(kernel, out_shape=jax.ShapeDtypeStruct((HEADS, 3, HALF, 2...]
    unnamed x7 -> x0, local copies, waits for them, and re-layouts: 3.7 us -> none
where the time goes in v2:
time: 61.1 us; the launch traced here: 61 us
  Pallas kernels  59.7 us (98%)
  between operations  1.29 us (2%)
    pallas_call x1, Pallas kernels, on_device(): pl.pallas_call(kernel, out_shape=jax.ShapeDtypeStruct((HEADS, 3, HALF, 2...  56.6 us
    pallas_call x1, Pallas kernels, on_device(): pl.pallas_call(finish, grid=(HEADS // 2 // PAIRS,), out_shape=[jax.ShapeD...  3.06 us

profile of v2, /device:TPU:1, one launch (start us, length us, event | category | flops | bytes accessed | tf_op | source)
XLA Modules:
  0.0 61.0 jit_solution(1963510068932073943)
XLA Ops:
  1.3 56.6 %shard_map.94.back = bf16[12,3,128,128]{3,2,1,0:T(8,128)(2,1)} custom-call(bf16[256,768]{1,0:T(8,128)(2,1)} %bitcast.8, bf16[256,768]{1,0:T(8,128)(2,1)} %bitcast.9, bf16[256,768]{1,0:T(8,128)(2,1)} %bitcast.10, bf16[256,768]{1,0:T(8,128)(2,1)} %bitcast.11, bf16[2,48,768]{2,1,0:T(8,128)(2,1)} %bitcast.15, s32[2,12]{1,0:T(2,128)} %off_ref.3, s32[1]{0:T(128)S(6)} %copy.10.valid_ref), custom_call_target="tpu_custom_call" | custom-call | flops 4000000000 | bytes 3000000 | tf_op jit(solution)/shard_map/pallas_call | solution.py:479
  57.9 3.1 %shard_map.95 = (bf16[256,768]{1,0:T(8,128)(2,1)}, bf16[256,768]{1,0:T(8,128)(2,1)}, bf16[256,768]{1,0:T(8,128)(2,1)}) custom-call(s32[2,12]{1,0:T(2,128)} %off_ref.3, bf16[12,3,128,128]{3,2,1,0:T(8,128)(2,1)} %shard_map.94.back), custom_call_target="tpu_custom_call" | custom-call | tf_op jit(solution)/shard_map/pallas_call | solution.py:517

commit v3 on v2

--- a/solution.py
+++ b/solution.py
@@ -50,7 +50,7 @@
 def kernel(
     q_in, k_in, v_in, og_in, w_ref, off_ref, valid_ref,
     back,
-    xin, qks, vs, gs, qk, vin, gin, vd, kp, kt, w4, ebuf, stat, dpbuf, dsp, acc, xsib, out, dqbuf, og_perm,
+    xin, qks, vs, gs, qk, vin, gin, vd, kp, kt, w4, ebuf, stat, dpbuf, dsp, acc, xsib, out, og_perm,
     w_send, w_recv, a_send, a_recv, f_send, f_recv, x_send, x_recv, o_send, o_recv,
     l_sem, in_sem,
 ):
@@ -127,32 +127,37 @@
     def pack_one(dst, x, tile):
         dst[2 * tile], dst[2 * tile + 1] = side_by_side(*classes(x, takes_odd(tile)))
 
-    def place(dst, slot, s):
+    def place(dst, slot, s, to_core):
+        s = s ^ (QUAD * to_core)
         return dst.at[slot, :, s] if len(dst.shape) == 5 else dst.at[slot, s]
 
     def full_copy(src, dst, which, d):
         p = m ^ d
         return remote(
-            src.at[full_head(p)], place(dst, 0, m), a_send.at[which], a_recv.at[which, 0], dev(p)
+            src.at[full_head(p)], place(dst, 0, m, p % 2), a_send.at[which], a_recv.at[which, 0], dev(p)
         )
 
     def shared_copy(src, dst, which, dx):
         to = chip ^ dx
         return remote(
-            src.at[3 * to + 1], place(dst, 1, m), a_send.at[which], a_recv.at[which, 1],
+            src.at[3 * to + 1], place(dst, 1, m, half), a_send.at[which], a_recv.at[which, 1],
             dev(2 * to + half),
         )
 
     def local_full(src, dst, which):
-        return pltpu.make_async_copy(src.at[full_head(m)], place(dst, 0, m), a_recv.at[which, 0])
+        return pltpu.make_async_copy(src.at[full_head(m)], place(dst, 0, m, core), a_recv.at[which, 0])
 
     def local_shared(src, dst, which):
-        return pltpu.make_async_copy(src.at[3 * chip + 1], place(dst, 1, m), a_recv.at[which, 1])
-
-    def exchange(src, dst, which):
-        for d in range(1, GROUP):
-            full_copy(src, dst, which, d).start()
-        local_full(src, dst, which).start()
+        return pltpu.make_async_copy(src.at[3 * chip + 1], place(dst, 1, m, half), a_recv.at[which, 1])
+
+    def exchange(src, dst, which, shared_first=False):
+        def send_full():
+            for d in range(1, GROUP):
+                full_copy(src, dst, which, d).start()
+            local_full(src, dst, which).start()
+
+        if not shared_first:
+            send_full()
         for dx in range(1, QUAD):
             shared_copy(src, dst, which, dx).start()
 
@@ -164,12 +169,14 @@
         def _():
             local_shared(src, dst, which).start()
 
+        if shared_first:
+            send_full()
+
     def wait_full(dst, which):
         arrived(dst.at[0], a_recv.at[which, 0])
 
     def wait_shared(dst, which):
-        part = pl.ds(QUAD * core, QUAD)
-        arrived(dst.at[1, :, part] if which == 0 else dst.at[1, part], a_recv.at[which, 1])
+        arrived(dst.at[1, :, 0:QUAD] if which == 0 else dst.at[1, 0:QUAD], a_recv.at[which, 1])
 
     def positions(row, cls, off):
         return base * ROWS + 2 * row + (off if cls == 0 else 1 - off)
@@ -178,14 +185,14 @@
     key_row = lax.broadcasted_iota(jnp.int32, (KC, 1), 0)
 
     def prepare(slot, cls, seg, off):
-        bias = jnp.where(positions(seg * KC + key_row, cls, off) < valid, 0.0, NEG)
-        x = qk[slot, cls, pl.ds(seg * QUAD, QUAD)].reshape(KC, 2 * HD).astype(F32)
-        rows = pl.ds(pl.multiple_of(seg * KC, KC), KC)
+        bias = jnp.where(positions((seg ^ core) * KC + key_row, cls, off) < valid, 0.0, NEG)
+        x = qk[slot, cls, seg * QUAD:(seg + 1) * QUAD].reshape(KC, 2 * HD).astype(F32)
+        rows = slice(seg * KC, (seg + 1) * KC)
         kp[slot, cls, rows] = jnp.where(wide >= HD, x, jnp.where(wide == 0, bias, 0.0)).astype(BF16)
         kt[slot, cls, :, rows] = jnp.transpose(x)[HD:].astype(BF16)
 
     def join(slot, cls, seg, with_grad):
-        part = pl.ds(seg * QUAD, QUAD)
+        part = slice(seg * QUAD, (seg + 1) * QUAD)
         x = vin[slot, part].reshape(KC, 2 * HD).astype(F32)
         g = 0.0
         if cls:
@@ -209,16 +216,16 @@
         return [(3, 0, c, 1), (4, 1, c, 1)]
 
     def scores(slot, off, c, i, cls):
-        b = 4 * slot + (2 * c + i if slot == 0 else i)
-        r0 = pl.multiple_of(c * KC + i * QB, QB)
-        xq = qk[slot, cls, pl.ds(c * QUAD + 2 * i, 2)].reshape(QB, 2 * HD).astype(F32)
+        b = 4 * slot + 2 * c + i
+        r0 = (c ^ core) * KC + i * QB
+        xq = qk[slot, cls, c * QUAD + 2 * i:c * QUAD + 2 * i + 2].reshape(QB, 2 * HD).astype(F32)
         use = jnp.where(positions(r0 + qrow, cls, off) < valid, 1.0, 0.0)
         qp = jnp.where(qlow, jnp.where(qlane == 0, use, 0.0), pltpu.roll(xq, HD, 1)).astype(BF16)
         chunks = chunks_of(c, cls)
         top = jnp.full((8, QB), -jnp.inf, F32)
         for n, kc, seg, mult in chunks:
             for u in range(KC // SUB):
-                s = nt(kp[slot, kc, pl.ds(pl.multiple_of(seg * KC + u * SUB, SUB), SUB)], qp)
+                s = nt(kp[slot, kc, seg * KC + u * SUB:seg * KC + (u + 1) * SUB], qp)
                 ebuf[b, n, u * SUB:(u + 1) * SUB] = s
                 top = jnp.maximum(top, fold(s, jnp.max))
         top = jnp.max(top, axis=0, keepdims=True)
@@ -231,74 +238,103 @@
                 total = total + mult * fold(e, jnp.sum)
         stat[b, cls] = 1.0 / jnp.sum(total, axis=0, keepdims=True)
 
-    def gradients(slot, c, i, cls):
-        b = 4 * slot + (2 * c + i if slot == 0 else i)
-        s0 = c * QUAD + 2 * i
-        xq = qk[slot, cls, pl.ds(s0, 2)].reshape(QB, 2 * HD).astype(F32)
-        xv = vd[slot, cls, pl.ds(s0, 2)].reshape(QB, 2 * HD).astype(F32)
-        gp = jnp.where(qlow, 0.0, xv)
-        g0 = gp.astype(BF16)
-        gp = pltpu.roll(gp, HD, 1).astype(BF16)
-        q0 = jnp.where(qlow, xq, 0.0).astype(BF16)
-        grads = jnp.concatenate([q0, g0], axis=0)
-        chunks = chunks_of(c, cls)
-        dot_sum = jnp.zeros((8, QB), F32)
-        for n, kc, seg, mult in chunks:
-            for u in range(KC // SUB):
-                su = slice(u * SUB, (u + 1) * SUB)
-                per = SUB // HALF
-                values = vd[slot, kc, pl.ds(seg * QUAD + u * per, per)].reshape(SUB, 2 * HD)
-                dp = nt(values, gp)
-                dpbuf[n, su] = dp
-                dot_sum = dot_sum + mult * fold(ebuf[b, n, su] * dp, jnp.sum)
-        inv = stat[b, cls]
-        delta = jnp.sum(dot_sum, axis=0, keepdims=True) * inv
-        dqt = jnp.zeros((HD, QB), F32)
-        for n, kc, seg, mult in chunks:
-            rows = pl.ds(pl.multiple_of(seg * KC, KC), KC)
-            for u in range(KC // SUB):
-                su = slice(u * SUB, (u + 1) * SUB)
-                p = ebuf[b, n, su] * inv
-                ds = p * (dpbuf[n, su] - delta)
-                dsp[n, su, :QB] = ds.astype(BF16)
-                dsp[n, su, QB:] = p.astype(BF16)
-            acc[slot, kc, rows] += nn(dsp[n], grads * mult if mult != 1 else grads)
-            keys_t = kt[slot, kc, :, rows]
-            dqt = dqt + nn(keys_t * mult if mult != 1 else keys_t, dsp[n, :, :QB])
-        return dqt
-
-    def put_dq(slot, s0, sel, oth):
-        dq = jnp.transpose(jnp.concatenate([sel, oth], axis=0)) * (HD ** -0.5)
-        out[slot, pl.ds(s0, 2), 2] = dq.reshape(2, HALF, 2 * HD).astype(BF16)
-
-    def send_out(slot, s, kind):
+    def send_out(slot, c, j, kind):
+        j = j ^ (m % QUAD)
         head = full_head(m) if slot == 0 else 3 * chip + 1
         return remote(
-            out.at[slot, s, kind], back.at[head, kind], o_send.at[0], o_recv.at[0], dev(s)
+            out.at[slot, QUAD * c + j, kind], back.at[head, kind], o_send.at[0], o_recv.at[0],
+            dev(QUAD * (c ^ core) + j),
         )
 
-    def keep_out(slot, kind):
+    def start_others(slot, c, kind):
+        for j in range(1, QUAD):
+            send_out(slot, c, j, kind).start()
+
+    def start_last(slot, c, kinds):
         head = full_head(m) if slot == 0 else 3 * chip + 1
-        return pltpu.make_async_copy(out.at[slot, m, kind], back.at[head, kind], o_recv.at[0])
-
-    def start_out(slot, s, kind):
-        @pl.when(s != m)
+
+        @pl.when((c ^ core) != half)
         def _():
-            send_out(slot, s, kind).start()
-
-        @pl.when(s == m)
+            for kind in kinds:
+                send_out(slot, c, 0, kind).start()
+
+        @pl.when((c ^ core) == half)
         def _():
-            keep_out(slot, kind).start()
-
-    mine = pl.ds(QUAD * core, QUAD)
-    theirs = pl.ds(QUAD * (1 - core), QUAD)
-
-    def pass_on(dst, which, part):
-        ref = dst.at[1, 0, part] if which == 0 else dst.at[1, part]
-        return remote(ref, ref, f_send.at[which], f_recv.at[which], dev(m ^ 1))
+            for kind in kinds:
+                pltpu.make_async_copy(
+                    out.at[slot, QUAD * c + m % QUAD, kind], back.at[head, kind], o_recv.at[0]
+                ).start()
+
+    def put_terms(slot, cls, c, x):
+        out[slot, QUAD * c:QUAD * (c + 1), cls] = x.reshape(QUAD, HALF, 2 * HD).astype(BF16)
+        start_others(slot, c, cls)
+
+    def segment(slot, c, order, take):
+        rows = {}
+        stats = {}
+        for cls in range(2):
+            for i in range(2):
+                b = 4 * slot + 2 * c + i
+                s0 = c * QUAD + 2 * i
+                xq = qk[slot, cls, s0:s0 + 2].reshape(QB, 2 * HD).astype(F32)
+                xv = vd[slot, cls, s0:s0 + 2].reshape(QB, 2 * HD).astype(F32)
+                g = jnp.where(qlow, 0.0, xv)
+                rows[cls, i] = jnp.concatenate([jnp.where(qlow, xq, 0.0).astype(BF16), g.astype(BF16)], axis=0)
+                gp = pltpu.roll(g, HD, 1).astype(BF16)
+                dot_sum = jnp.zeros((8, QB), F32)
+                for n, kc, seg, mult in chunks_of(c, cls):
+                    for u in range(KC // SUB):
+                        su = slice(u * SUB, (u + 1) * SUB)
+                        per = SUB // HALF
+                        s1 = seg * QUAD + u * per
+                        dp = nt(vd[slot, kc, s1:s1 + per].reshape(SUB, 2 * HD), gp)
+                        dpbuf[i, n, su] = dp
+                        dot_sum = dot_sum + mult * fold(ebuf[b, n, su] * dp, jnp.sum)
+                inv = stat[b, cls]
+                stats[cls, i] = (inv, jnp.sum(dot_sum, axis=0, keepdims=True) * inv)
+        dqt = {}
+        for kc, seg in order:
+            terms = None
+            for cls in range(2):
+                for n, kn, sn, mult in chunks_of(c, cls):
+                    if (kn, sn) != (kc, seg):
+                        continue
+                    keys_t = kt[slot, kc, :, seg * KC:(seg + 1) * KC]
+                    keys_t = keys_t * mult if mult != 1 else keys_t
+                    for i in range(2):
+                        b = 4 * slot + 2 * c + i
+                        inv, delta = stats[cls, i]
+                        for u in range(KC // SUB):
+                            su = slice(u * SUB, (u + 1) * SUB)
+                            p = ebuf[b, n, su] * inv
+                            ds = p * (dpbuf[i, n, su] - delta)
+                            dsp[i, n, su, :QB] = ds.astype(BF16)
+                            dsp[i, n, su, QB:] = p.astype(BF16)
+                        g = rows[cls, i] * mult if mult != 1 else rows[cls, i]
+                        t = nn(dsp[i, n], g)
+                        terms = t if terms is None else terms + t
+                        t = nn(keys_t, dsp[i, n, :, :QB])
+                        dqt[cls, i] = dqt[cls, i] + t if (cls, i) in dqt else t
+            take(kc, seg, terms)
+        for i in range(2):
+            s0 = QUAD * c + 2 * i
+            dq = jnp.transpose(jnp.concatenate([dqt[0, i], dqt[1, i]], axis=0)) * (HD ** -0.5)
+            out[slot, s0:s0 + 2, 2] = dq.reshape(2, HALF, 2 * HD).astype(BF16)
+        start_others(slot, c, 2)
+
+    first, other = slice(0, QUAD), slice(QUAD, GROUP)
+
+    def pass_on(dst, which):
+        src, to = (dst.at[1, 0, first], dst.at[1, 0, other]) if which == 0 else (dst.at[1, first], dst.at[1, other])
+        return remote(src, to, f_send.at[which], f_recv.at[which], dev(m ^ 1))
 
     off0 = off_ref[1, full_head(m)]
     off1 = off_ref[1, 3 * chip + 1]
+
+    pl.semaphore_wait(barrier, GROUP - 1 + 4)
+    for n in range(2):
+        for way in range(2):
+            w_copy(way, 1, n, True)[1].start()
 
     perm = row_perm(1.0)
     perm_q = row_perm(HD ** -0.5)
@@ -307,10 +343,6 @@
     for t in range(HEADS // 2):
         cols = slice(t * 128, (t + 1) * 128)
         pack_pair(qks, nn(perm_q, xin[0, :, cols]), nn(perm, xin[1, :, cols]), t)
-    pl.semaphore_wait(barrier, GROUP - 1 + 4)
-    for n in range(2):
-        for way in range(2):
-            w_copy(way, 1, n, True)[1].start()
     exchange(qks, qk, 0)
 
     loads[2].wait()
@@ -320,7 +352,6 @@
 
     loads[3].wait()
     og_perm[...] = nn(perm, xin[3]).astype(BF16)
-    acc[...] = jnp.zeros_like(acc)
     for step in range(1, 4):
         for n in range(2):
             for way in range(2):
@@ -338,8 +369,7 @@
         for seg in range(2):
             prepare(0, cls, seg, off0)
 
-    @pl.loop(0, EARLY)
-    def _(t):
+    for t in range(EARLY):
         for cls in range(2):
             scores(0, off0, t // 2, t % 2, cls)
 
@@ -356,82 +386,73 @@
     for t in range(HEADS // 2):
         cols = slice(t * 128, (t + 1) * 128)
         pack_one(gs, grad[:, cols], t)
-    exchange(gs, gin, 2)
+    exchange(gs, gin, 2, shared_first=True)
 
     wait_shared(qk, 0)
-    pass_on(qk, 0, mine).start()
-
-    @pl.loop(EARLY, 4)
-    def _(t):
+    pass_on(qk, 0).start()
+
+    for t in range(EARLY, 4):
         for cls in range(2):
             scores(0, off0, t // 2, t % 2, cls)
 
-    pass_on(qk, 0, theirs).wait_recv()
+    pass_on(qk, 0).wait_recv()
     prepare(1, 0, 0, off1)
     prepare(1, 0, 1, off1)
-    prepare(1, 1, core, off1)
-
-    @pl.loop(0, 2)
-    def _(t):
+    prepare(1, 1, 0, off1)
+
+    for t in range(2):
         for cls in range(2):
-            scores(1, off1, core, t, cls)
-
-    def segment(slot, c, middle):
-        @pl.loop(0, 2)
-        def _(i):
-            dqbuf[i] = gradients(slot, c, i, 0)
-
-        middle()
-
-        @pl.loop(0, 2)
-        def _(i):
-            s0 = QUAD * c + 2 * i
-            put_dq(slot, s0, dqbuf[i], gradients(slot, c, i, 1))
-            for e in range(2):
-                start_out(slot, s0 + e, 2)
-
-    def send_terms(slot, cls, c, extra=None):
-        x = acc[slot, cls, pl.ds(pl.multiple_of(c * KC, KC), KC)]
-        if extra is not None:
-            x = x + extra
-        out[slot, pl.ds(QUAD * c, QUAD), cls] = x.reshape(QUAD, HALF, 2 * HD).astype(BF16)
-        for j in range(QUAD):
-            start_out(slot, QUAD * c + j, cls)
-
-    def swap_terms(c):
-        rows = pl.ds(pl.multiple_of(c * KC, KC), KC)
-        return remote(acc.at[1, 0, rows], xsib, x_send.at[0], x_recv.at[0], dev(m ^ 1))
+            scores(1, off1, 0, t, cls)
+
+    swap_terms = remote(acc.at[0], xsib, x_send.at[0], x_recv.at[0], dev(m ^ 1))
+
+    def take_shared(kc, seg, x):
+        if kc:
+            put_terms(1, 1, 0, x)
+        elif seg:
+            acc[0] = x
+            swap_terms.start()
+        else:
+            swap_terms.wait_recv()
+            put_terms(1, 0, 0, x + xsib[...])
+
+    def take_first(kc, seg, x):
+        if kc:
+            put_terms(0, 1, 0, x)
+        else:
+            acc[1 + seg] = x
+
+    def take_second(kc, seg, x):
+        put_terms(0, kc, seg, x if kc else x + acc[1 + seg])
 
     wait_shared(vin, 1)
-    pass_on(vin, 1, mine).start()
+    pass_on(vin, 1).start()
     wait_shared(gin, 2)
-    join(1, 0, core, True)
-    join(1, 1, core, True)
-    pass_on(vin, 1, theirs).wait_recv()
-    join(1, 0, 1 - core, False)
-    segment(1, core, lambda: swap_terms(1 - core).start())
-    send_terms(1, 1, core)
-    swap_terms(core).wait_recv()
-    send_terms(1, 0, core, xsib[...])
+    join(1, 0, 0, True)
+    join(1, 1, 0, True)
+    pass_on(vin, 1).wait_recv()
+    join(1, 0, 1, False)
+    segment(1, 0, ((0, 1), (1, 0), (0, 0)), take_shared)
+    start_last(1, 0, (1, 0, 2))
 
     wait_full(vin, 1)
     wait_full(gin, 2)
     for cls in range(2):
         for c in range(2):
             join(0, cls, c, True)
-    segment(0, core, lambda: None)
-    send_terms(0, 1, core)
-    segment(0, 1 - core, lambda: send_terms(0, 0, core))
-    send_terms(0, 1, 1 - core)
-    send_terms(0, 0, 1 - core)
+    segment(0, 0, ((1, 0), (0, 0), (0, 1)), take_first)
+    start_last(0, 0, (1, 2))
+    segment(0, 1, ((0, 0), (0, 1), (1, 1)), take_second)
+    start_last(0, 0, (0,))
+    start_last(0, 1, (0, 1, 2))
 
     arrived(back, o_recv.at[0])
 
     arrived(w4.at[pl.ds(0, nz - 1), 0], w_send.at[0])
     arrived(w4.at[pl.ds(0, nz - 1), 0], w_send.at[1])
-    swap_terms(1 - core).wait_send()
-    pass_on(qk, 0, mine).wait_send()
-    pass_on(vin, 1, mine).wait_send()
+    swap_terms.wait_send()
+    pass_on(qk, 0).wait_send()
+    pass_on(vin, 1).wait_send()
 
     def all_left(blocks):
         for which, src in enumerate((qks, vs, gs)):
@@ -460,8 +481,8 @@
             rows = jnp.concatenate([jnp.where(odd, oth, sel), jnp.where(odd, sel, oth)], axis=0)
             ref[:, cols] = nn(unperm, rows.astype(BF16)).astype(BF16)
 
-        one = [back[2 * t, n].astype(F32) for n in range(3)]
-        two = [back[2 * t + 1, n].astype(F32) for n in range(3)]
+        one = [back[2 * (first + t), n].astype(F32) for n in range(3)]
+        two = [back[2 * (first + t) + 1, n].astype(F32) for n in range(3)]
         left = [jnp.where(low, one[n], pltpu.roll(two[n], HD, 1)) for n in range(3)]
         right = [jnp.where(low, pltpu.roll(one[n], HD, 1), two[n]) for n in range(3)]
         put(dk_ref, left[0], left[1])
@@ -478,9 +499,9 @@
     dma = pltpu.SemaphoreType.DMA
     back = pl.pallas_call(
         kernel,
-        out_shape=jax.ShapeDtypeStruct((HEADS, 3, HALF, 2 * HD), BF16),
+        out_shape=pltpu.VMEM((HEADS, 3, HALF, 2 * HD), BF16),
         in_specs=[far] * 5 + [smem] * 2,
-        out_specs=far,
+        out_specs=pl.BlockSpec(memory_space=pltpu.VMEM),
         scratch_shapes=[
             pltpu.VMEM((4, ROWS, width), BF16),
             pltpu.VMEM((HEADS, 2, HALF, 2 * HD), BF16),
@@ -495,12 +516,11 @@
             pltpu.VMEM((nz, 2, w_rows, width), BF16),
             pltpu.VMEM((BLOCKS, 5, KC, QB), F32),
             pltpu.VMEM((BLOCKS, 2, 1, QB), F32),
-            pltpu.VMEM((5, KC, QB), F32),
-            pltpu.VMEM((5, KC, 2 * QB), BF16),
-            pltpu.VMEM((2, 2, SEG, 2 * HD), F32),
+            pltpu.VMEM((2, 5, KC, QB), F32),
+            pltpu.VMEM((2, 5, KC, 2 * QB), BF16),
+            pltpu.VMEM((3, KC, 2 * HD), F32),
             pltpu.VMEM((KC, 2 * HD), F32),
             pltpu.VMEM((2, GROUP, 3, HALF, 2 * HD), BF16),
-            pltpu.VMEM((2, HD, QB), F32),
             pltpu.VMEM((ROWS, width), BF16),
             dma((2,)), dma((17,)), dma((3,)), dma((3, 2)),
             dma((2,)), dma((2,)), dma((1,)), dma((1,)), dma((1,)), dma((1,)), dma((1,)), dma((4,)),
@@ -514,11 +534,12 @@
         w_out.reshape(2, w_rows, width), head_offsets, valid_tiles,
     )
     columns = pl.BlockSpec((ROWS, PAIRS * 2 * HD), lambda t: (0, t))
+    back = pltpu.with_memory_space_constraint(back, pltpu.VMEM)
     outs = pl.pallas_call(
         finish,
         grid=(HEADS // 2 // PAIRS,),
         out_shape=[jax.ShapeDtypeStruct((ROWS, width), BF16)] * 3,
-        in_specs=[smem, pl.BlockSpec((2 * PAIRS, 3, HALF, 2 * HD), lambda t: (t, 0, 0, 0))],
+        in_specs=[smem, pl.BlockSpec(memory_space=pltpu.VMEM)],
         out_specs=[columns] * 3,
     )(head_offsets, back)
     return tuple(o[None] for o in outs)

time: 61.1 us -> 56.1 us (0.918)
  Pallas kernels: 59.7 us -> 54.6 us
    pallas_call x1, Pallas kernels: 56.6 us -> 51.9 us  [on_device(): pl.pallas_call(kernel, out_shape=pltpu.VMEM((HEADS, 3, HALF, 2 * HD), BF1...]
where the time goes in v3:
time: 56.1 us; the launch traced here: 55.9 us
  Pallas kernels  54.6 us (97%)
  between operations  1.29 us (2%)
    pallas_call x1, Pallas kernels, on_device(): pl.pallas_call(kernel, out_shape=pltpu.VMEM((HEADS, 3, HALF, 2 * HD), BF1...  51.9 us
    pallas_call x1, Pallas kernels, on_device(): pl.pallas_call(finish, grid=(HEADS // 2 // PAIRS,), out_shape=[jax.ShapeD...  2.69 us

profile of v3, /device:TPU:1, one launch (start us, length us, event | category | flops | bytes accessed | tf_op | source)
XLA Modules:
  0.0 55.9 jit_solution(11784482334984410881)
XLA Ops:
  1.3 51.9 %shard_map.94.back = bf16[12,3,128,128]{3,2,1,0:T(8,128)(2,1)S(1)} custom-call(bf16[256,768]{1,0:T(8,128)(2,1)} %bitcast.8, bf16[256,768]{1,0:T(8,128)(2,1)} %bitcast.9, bf16[256,768]{1,0:T(8,128)(2,1)} %bitcast.10, bf16[256,768]{1,0:T(8,128)(2,1)} %bitcast.11, bf16[2,48,768]{2,1,0:T(8,128)(2,1)} %bitcast.15, s32[2,12]{1,0:T(2,128)} %off_ref.3, ...), custom_call_target="tpu_custom_call" | custom-call | flops 4000000000 | bytes 3000000 | tf_op jit(solution)/shard_map/pallas_call | solution.py:500
  53.2 2.7 %shard_map.95 = (bf16[256,768]{1,0:T(8,128)(2,1)}, bf16[256,768]{1,0:T(8,128)(2,1)}, bf16[256,768]{1,0:T(8,128)(2,1)}) custom-call(s32[2,12]{1,0:T(2,128)} %off_ref.3, bf16[12,3,128,128]{3,2,1,0:T(8,128)(2,1)S(1)} %shard_map.94.back), custom_call_target="tpu_custom_call" | custom-call | tf_op jit(solution)/shard_map/pallas_call | solution.py:538

commit v4 on v3

--- a/solution.py
+++ b/solution.py
@@ -52,7 +52,7 @@
     back,
     xin, qks, vs, gs, qk, vin, gin, vd, kp, kt, w4, ebuf, stat, dpbuf, dsp, acc, xsib, out, og_perm,
     w_send, w_recv, a_send, a_recv, f_send, f_recv, x_send, x_recv, o_send, o_recv,
-    l_sem, in_sem,
+    l_sem, in_sem, ready,
 ):
     ctx = lax.axis_index("ctx")
     z = lax.axis_index("fsdp")
@@ -75,11 +75,25 @@
     def full_head(p):
         return 3 * (p // 2) + 2 * (p % 2)
 
+    upper = z >= nz // 2
     barrier = pltpu.get_barrier_semaphore()
-    for d in range(1, GROUP):
-        pl.semaphore_signal(barrier, inc=1, device_id=dev(m ^ d), device_id_type=MESH)
+    for dx in range(1, QUAD):
+        pl.semaphore_signal(barrier, inc=1, device_id=dev(2 * (chip ^ dx)), device_id_type=MESH)
+
+    @pl.when(jnp.logical_or(core == 1, upper))
+    def _():
+        pl.semaphore_signal(barrier, inc=1, device_id=dev(m ^ 1), device_id_type=MESH)
+
+    @pl.when(upper)
+    def _():
+        for dx in range(1, QUAD):
+            pl.semaphore_signal(barrier, inc=1, device_id=dev(2 * (chip ^ dx) + 1), device_id_type=MESH)
+
     for d in (1, 2, nz - 2, nz - 1):
-        pl.semaphore_signal(barrier, inc=1, device_id=(ctx, (z + d) % nz), device_id_type=MESH)
+        to = (z + d) % nz
+        pl.semaphore_signal(
+            barrier, inc=1, device_id=(base + 2 * chip + jnp.where(to >= nz // 2, core, 1), to), device_id_type=MESH
+        )
     loads = [pltpu.make_async_copy(x, xin.at[n], in_sem.at[n]) for n, x in enumerate((q_in, k_in, v_in, og_in))]
     for c in loads:
         c.start()
@@ -331,10 +345,20 @@
     off0 = off_ref[1, full_head(m)]
     off1 = off_ref[1, 3 * chip + 1]
 
-    pl.semaphore_wait(barrier, GROUP - 1 + 4)
-    for n in range(2):
-        for way in range(2):
-            w_copy(way, 1, n, True)[1].start()
+    def first_w():
+        for n in range(2):
+            for way in range(2):
+                w_copy(way, 1, n, True)[1].start()
+
+    @pl.when(upper)
+    def _():
+        pl.semaphore_wait(barrier, GROUP - 1 + 4)
+        first_w()
+
+    @pl.when(jnp.logical_and(core == 0, jnp.logical_not(upper)))
+    def _():
+        pl.semaphore_wait(barrier, GROUP - 1)
+        pl.semaphore_signal(ready, inc=1, device_id=dev(m ^ 1), device_id_type=MESH)
 
     perm = row_perm(1.0)
     perm_q = row_perm(HD ** -0.5)
@@ -343,7 +367,24 @@
     for t in range(HEADS // 2):
         cols = slice(t * 128, (t + 1) * 128)
         pack_pair(qks, nn(perm_q, xin[0, :, cols]), nn(perm, xin[1, :, cols]), t)
+    @pl.when(jnp.logical_and(core == 1, jnp.logical_not(upper)))
+    def _():
+        pl.semaphore_wait(ready, 1)
+
     exchange(qks, qk, 0)
+
+    @pl.when(jnp.logical_not(upper))
+    def _():
+        @pl.when(core == 1)
+        def _():
+            pl.semaphore_wait(barrier, 2 * 4)
+            pl.semaphore_signal(ready, inc=1, device_id=dev(m ^ 1), device_id_type=MESH)
+
+        @pl.when(core == 0)
+        def _():
+            pl.semaphore_wait(ready, 1)
+
+        first_w()
 
     loads[2].wait()
     for t in range(HEADS // 2):
@@ -399,6 +440,8 @@
     prepare(1, 0, 0, off1)
     prepare(1, 0, 1, off1)
     prepare(1, 1, 0, off1)
+    wait_shared(vin, 1)
+    pass_on(vin, 1).start()
 
     for t in range(2):
         for cls in range(2):
@@ -425,13 +468,11 @@
     def take_second(kc, seg, x):
         put_terms(0, kc, seg, x if kc else x + acc[1 + seg])
 
-    wait_shared(vin, 1)
-    pass_on(vin, 1).start()
+    pass_on(vin, 1).wait_recv()
+    join(1, 0, 1, False)
     wait_shared(gin, 2)
     join(1, 0, 0, True)
     join(1, 1, 0, True)
-    pass_on(vin, 1).wait_recv()
-    join(1, 0, 1, False)
     segment(1, 0, ((0, 1), (1, 0), (0, 0)), take_shared)
     start_last(1, 0, (1, 0, 2))
 
@@ -524,6 +565,7 @@
             pltpu.VMEM((ROWS, width), BF16),
             dma((2,)), dma((17,)), dma((3,)), dma((3, 2)),
             dma((2,)), dma((2,)), dma((1,)), dma((1,)), dma((1,)), dma((1,)), dma((1,)), dma((4,)),
+            pltpu.SemaphoreType.REGULAR,
         ],
         compiler_params=pltpu.CompilerParams(
             collective_id=0, has_side_effects=True, vmem_limit_bytes=56 * 1024 * 1024

time: 56.1 us -> 56.3 us (level)
  no operation moved by 1% of the time
where the time goes in v4:
time: 56.3 us; the launch traced here: 56.1 us
  Pallas kernels  54.8 us (97%)
  between operations  1.29 us (2%)
    pallas_call x1, Pallas kernels, on_device(): pl.pallas_call(kernel, out_shape=pltpu.VMEM((HEADS, 3, HALF, 2 * HD), BF1...  52.1 us
    pallas_call x1, Pallas kernels, on_device(): pl.pallas_call(finish, grid=(HEADS // 2 // PAIRS,), out_shape=[jax.ShapeD...  2.68 us

profile of v4, /device:TPU:1, one launch (start us, length us, event | category | flops | bytes accessed | tf_op | source)
XLA Modules:
  0.0 56.1 jit_solution(2746561513884797744)
XLA Ops:
  1.3 52.1 %shard_map.94.back = bf16[12,3,128,128]{3,2,1,0:T(8,128)(2,1)S(1)} custom-call(bf16[256,768]{1,0:T(8,128)(2,1)} %bitcast.8, bf16[256,768]{1,0:T(8,128)(2,1)} %bitcast.9, bf16[256,768]{1,0:T(8,128)(2,1)} %bitcast.10, bf16[256,768]{1,0:T(8,128)(2,1)} %bitcast.11, bf16[2,48,768]{2,1,0:T(8,128)(2,1)} %bitcast.15, s32[2,12]{1,0:T(2,128)} %off_ref.3, ...), custom_call_target="tpu_custom_call" | custom-call | flops 4000000000 | bytes 3000000 | tf_op jit(solution)/shard_map/pallas_call | solution.py:541
  53.4 2.7 %shard_map.95 = (bf16[256,768]{1,0:T(8,128)(2,1)}, bf16[256,768]{1,0:T(8,128)(2,1)}, bf16[256,768]{1,0:T(8,128)(2,1)}) custom-call(s32[2,12]{1,0:T(2,128)} %off_ref.3, bf16[12,3,128,128]{3,2,1,0:T(8,128)(2,1)S(1)} %shard_map.94.back), custom_call_target="tpu_custom_call" | custom-call | tf_op jit(solution)/shard_map/pallas_call | solution.py:580

commit v5 on v4

--- a/solution.py
+++ b/solution.py
@@ -16,8 +16,8 @@
 KC = 512
 SUB = 256
 NEG = -1e30
-PAIRS = 3
-EARLY = 2
+PAIRS = 6
+EARLY = 1
 W_CUT = 32
 BLOCKS = 6
 F32 = jnp.float32
@@ -473,7 +473,7 @@
     wait_shared(gin, 2)
     join(1, 0, 0, True)
     join(1, 1, 0, True)
-    segment(1, 0, ((0, 1), (1, 0), (0, 0)), take_shared)
+    segment(1, 0, ((1, 0), (0, 1), (0, 0)), take_shared)
     start_last(1, 0, (1, 0, 2))
 
     wait_full(vin, 1)

time: 56.3 us -> 55.9 us (level)
  no operation moved by 1% of the time
where the time goes in v5:
time: 55.9 us; the launch traced here: 55.8 us
  Pallas kernels  54.5 us (97%)
  between operations  1.29 us (2%)
    pallas_call x1, Pallas kernels, on_device(): pl.pallas_call(kernel, out_shape=pltpu.VMEM((HEADS, 3, HALF, 2 * HD), BF1...  51.9 us
    pallas_call x1, Pallas kernels, on_device(): pl.pallas_call(finish, grid=(HEADS // 2 // PAIRS,), out_shape=[jax.ShapeD...  2.6 us

profile of v5, /device:TPU:1, one launch (start us, length us, event | category | flops | bytes accessed | tf_op | source)
XLA Modules:
  0.0 55.8 jit_solution(15419677784956618300)
XLA Ops:
  1.3 51.9 %shard_map.94.back = bf16[12,3,128,128]{3,2,1,0:T(8,128)(2,1)S(1)} custom-call(bf16[256,768]{1,0:T(8,128)(2,1)} %bitcast.8, bf16[256,768]{1,0:T(8,128)(2,1)} %bitcast.9, bf16[256,768]{1,0:T(8,128)(2,1)} %bitcast.10, bf16[256,768]{1,0:T(8,128)(2,1)} %bitcast.11, bf16[2,48,768]{2,1,0:T(8,128)(2,1)} %bitcast.15, s32[2,12]{1,0:T(2,128)} %off_ref.3, ...), custom_call_target="tpu_custom_call" | custom-call | flops 4000000000 | bytes 3000000 | tf_op jit(solution)/shard_map/pallas_call | solution.py:541
  53.1 2.6 %shard_map.95 = (bf16[256,768]{1,0:T(8,128)(2,1)}, bf16[256,768]{1,0:T(8,128)(2,1)}, bf16[256,768]{1,0:T(8,128)(2,1)}) custom-call(s32[2,12]{1,0:T(2,128)} %off_ref.3, bf16[12,3,128,128]{3,2,1,0:T(8,128)(2,1)S(1)} %shard_map.94.back), custom_call_target="tpu_custom_call" | custom-call | tf_op jit(solution)/shard_map/pallas_call | solution.py:580
